TPU v7x, 512 devices: a whole 4x4x16 slice. The times are simulated.
512 devices in a mesh: grp: 8 (over y, core), dev: 64 (over x, z).
Axes of the slice: x: 4, y: 4, z: 16, core: 2. Of those that a mesh axis runs over, the one named last changes fastest.
Arguments:
- tiles: bfloat16 [8, 3456, 64, 64], P('grp', 'dev'), may hold values from -0.15625 to 0.15625
- owner: int32 [8, 3456, 1], P('grp', 'dev'), may hold values from 0 to 63; in each aligned block of 54 rows (0 to 53, 54 to 107, ..., all dimensions but the last counted through in order) at most 2 rows name the same one
- tile_rows: int32 [8, 3456], P('grp', 'dev'), may hold values from 0 to 1
- tile_cols: int32 [8, 3456], P('grp', 'dev'), may hold values from 0 to 3
- ghost_rows: int32 [8, 128], P('grp', 'dev'), may hold values from 0 to 1
- rhs: float32 [8, 32, 8192], P('grp', None, 'dev')
- start: float32 [8, 32, 8192], P('grp', None, 'dev'), may hold values from -3 to 3
- diag: float32 [8, 8192], P('grp', 'dev'), may hold values from 2 to 20
Outputs:
- smoothed: float32 [8, 32, 8192], P('grp', None, 'dev')
- residual_rms: float32 [32], replicated
Inputs may be any that keep to these rules, and one draw needn't show every extreme that they name: Among the 54 tiles held by one device, no owner is named more than 2 times, a bound that some block reaches.
All inputs are finite; a program needn't handle non-finite values.
Results may differ from a plain program's by a relative error of at most 0.0013.
Values may be sent and summed in bfloat16 or wider, within the bound.
A program may use at most 64 MiB of HBM per device.

v0:
```python
import jax
import jax.numpy as jnp
from jax import lax
from jax.sharding import PartitionSpec as P

STEPS = 3


def from_behind(value, axis, steps):
    count = lax.axis_size(axis)
    initial, last = (max(0, -steps), min(count, count - steps))
    return lax.ppermute(value, axis, [(source, source + steps) for source in range(initial, last)])


def build_slots(owner_col, peers_count, cap):
    peers = jnp.arange(peers_count, dtype=jnp.int32)
    hits = (owner_col[:, None] == peers[None, :]).astype(jnp.int32)
    ranks = jnp.sum((jnp.cumsum(hits, axis=0) - 1) * hits, axis=1)
    return owner_col * cap + ranks


def ghost_extend(low, ghost_idx, half):
    packed = low[:, ghost_idx, :]
    lower_part = packed[:, :half]
    upper_part = packed[:, half:]
    from_lower = from_behind(upper_part, "dev", 1)
    from_upper = from_behind(lower_part, "dev", -1)
    return jnp.concatenate([low, from_lower, from_upper], axis=1)


def shards(tiles, owner, tile_rows, tile_cols, ghost_rows, rhs, start, diag):
    peers_count = lax.axis_size("dev")
    tile_count = tiles.shape[1]
    block = tiles.shape[2]
    width = rhs.shape[1]
    rows_own = rhs.shape[2] // block
    half = ghost_rows.shape[1] // 2
    columns = rows_own + 2 * half
    cap = 2 * ((tile_count + peers_count - 1) // peers_count)
    slot_total = peers_count * cap
    slots = build_slots(owner[0, :, 0], peers_count, cap)
    place = tile_rows[0] * columns + tile_cols[0]
    sent_tiles = (
        jnp.zeros((slot_total, block, block), jnp.bfloat16)
        .at[slots]
        .set(tiles[0])
        .reshape(peers_count, cap, block, block)
    )
    sent_place = (
        jnp.full((slot_total,), -1, jnp.int32).at[slots].set(place).reshape(peers_count, cap)
    )
    got_tiles, got_place = (
        lax.all_to_all(sent_tiles, "dev", split_axis=0, concat_axis=0, tiled=True),
        lax.all_to_all(sent_place, "dev", split_axis=0, concat_axis=0, tiled=True),
    )
    matrix = got_tiles.reshape(slot_total, block, block)
    places = got_place.reshape(slot_total)
    dest_rows = places // columns
    dest_cols = jnp.where(places >= 0, places % columns, 0)
    row_onehot = (dest_rows[:, None] == jnp.arange(rows_own, dtype=jnp.int32)[None, :]).astype(
        jnp.float32
    )
    ghost_idx = ghost_rows[0]
    diag_blocks = diag[0].reshape(1, rows_own, block)

    def apply_op(vec):
        extended = ghost_extend(vec.astype(jnp.bfloat16), ghost_idx, half)
        picked = extended[:, dest_cols, :]
        products = jnp.einsum("sij,rsj->sri", matrix, picked, preferred_element_type=jnp.float32)
        summed = jnp.einsum("sri,sb->rbi", products, row_onehot, precision=lax.Precision.HIGHEST)
        return diag_blocks * vec + summed

    lmax = 2.0
    lmin = 0.2
    theta = (lmax + lmin) / 2.0
    delta = (lmax - lmin) / 2.0
    sigma = theta / delta
    right = rhs[0].reshape(width, rows_own, block)
    iterate = start[0].reshape(width, rows_own, block)
    residual = right - apply_op(iterate)
    direction = residual / (theta * diag_blocks)
    rho = 1.0 / sigma
    for step in range(STEPS):
        iterate = iterate + direction
        residual = residual - apply_op(direction)
        if step + 1 < STEPS:
            rho_new = 1.0 / (2.0 * sigma - rho)
            direction = rho_new * rho * direction + 2.0 * rho_new / delta * residual / diag_blocks
            rho = rho_new
    squares = lax.psum(jnp.sum(residual * residual, axis=(1, 2)), ("grp", "dev"))
    unknowns = lax.axis_size("grp") * peers_count * rows_own * block
    residual_rms = jnp.sqrt(squares / unknowns)
    return (iterate.reshape(1, width, rows_own * block), residual_rms)


def solution(mesh):
    return jax.shard_map(
        shards,
        mesh=mesh,
        in_specs=(
            P("grp", "dev", None, None),
            P("grp", "dev", None),
            P("grp", "dev"),
            P("grp", "dev"),
            P("grp", "dev"),
            P("grp", None, "dev"),
            P("grp", None, "dev"),
            P("grp", "dev"),
        ),
        out_specs=(P("grp", None, "dev"), P()),
        check_vma=False,
    )
```

profile of v0, /device:TPU:1, one launch (start us, length us, event | category | flops | bytes accessed | tf_op | source)
XLA Modules:
  0.0 252.5 jit_solution(15945817437166856779)
XLA Ops:
  0.6 0.8 fusion.22
  1.4 0.1 reduce_window_sum.11
  1.5 0.8 select_reduce_fusion
  2.4 0.7 fusion.29
  3.0 0.7 add_bitcast_fusion
  3.7 0.7 scatter_custom_fusion
  4.5 0.7 all_to_all.9
  5.2 19.1 %all-to-all-start = ((s32[64,1,2]{2,1,0:T(1,128)}), s32[64,1,2]{2,1,0:T(1,128)S(1)}, u32[]{:S(2)}, u32[]{:S(2)}) async-start(s32[64,1,2]{2,1,0:T(1,128)} %bitcast.5), calls=%async_computation | async-start | bytes 65536 | tf_op jit(solution)/shard_map/all_to_all | solution.py:54
  24.3 0.5 broadcast_in_dim.7
  24.9 2.9 %scatter_fusion = bf16[128,64,64]{2,1,0:T(8,128)(2,1)S(1)} fusion(bf16[128,64,64]{2,1,0:T(8,128)(2,1)S(1)} %broadcast_in_dim.7, s32[54]{0:T(128)S(1)} %fusion.29, bf16[54,64,64]{2,1,0:T(8,128)(2,1)S(1)} %bitcast.103), kind=kCustom, calls=%fused_computation.9 | custom fusion | bytes 1327320 | tf_op jit(solution)/shard_map/scatter | solution.py:46
  27.8 0.0 copy-start.1
  27.8 0.0 copy-start.3
  27.8 0.0 copy-start.4
  27.8 0.0 copy-start.2
  27.8 2.3 reshape.302
  30.1 7.4 %all-to-all-done = s32[64,1,2]{2,1,0:T(1,128)S(1)} async-done(((s32[64,1,2]{2,1,0:T(1,128)}), s32[64,1,2]{2,1,0:T(1,128)S(1)}, u32[]{:S(2)}, u32[]{:S(2)}) %all-to-all-start) | async-done | bytes 544 | tf_op jit(solution)/shard_map/all_to_all | solution.py:54
  37.5 7.5 %all-to-all-start.1 = ((bf16[64,2,4096]{2,1,0:T(2,128)(2,1)}), bf16[64,2,4096]{2,1,0:T(2,128)(2,1)}, u32[]{:S(2)}, u32[]{:S(2)}) async-start(bf16[64,2,4096]{2,1,0:T(2,128)(2,1)} %reshape.302), calls=%async_computation.1 | async-start | bytes 2097152 | tf_op jit(solution)/shard_map/all_to_all | solution.py:53
  45.0 0.1 reshape_squeeze.7
  45.1 0.6 gather_fusion
  45.7 2.8 %collective-permute-start = (bf16[32,1,64]{2,0,1:T(8,128)(2,1)S(1)}, bf16[32,1,64]{2,0,1:T(8,128)(2,1)S(1)}, u32[]{:S(2)}, u32[]{:S(2)}) collective-permute-start(bf16[32,1,64]{2,0,1:T(8,128)(2,1)S(1)} %get-tuple-element.12), channel_id=1, source_target_pairs={{0,1},{1,2},{2,3},{3,4},{4,5},{5,6},{6,7},{7,8},{8,9},{9,10},{10,1... | collective-permute-start | bytes 12296 | tf_op jit(solution)/shard_map/ppermute | solution.py:12
  48.5 1.3 collective-permute-start.1
  49.8 0.5 broadcast.210
  50.3 0.7 reduce.9
  51.0 0.1 mul.92
  51.1 0.1 reshape_squeeze.8
  51.2 0.1 reshape.194
  51.3 0.5 broadcast.209
  51.8 0.7 reduce.8
  52.6 0.1 reshape.193
  52.7 25.1 %collective-permute-done = bf16[32,1,64]{2,0,1:T(8,128)(2,1)S(1)} collective-permute-done((bf16[32,1,64]{2,0,1:T(8,128)(2,1)S(1)}, bf16[32,1,64]{2,0,1:T(8,128)(2,1)S(1)}, u32[]{:S(2)}, u32[]{:S(2)}) %collective-permute-start) | collective-permute-done | bytes 4128 | tf_op jit(solution)/shard_map/ppermute | solution.py:12
  77.9 9.6 %collective-permute-done.1 = bf16[32,1,64]{2,0,1:T(8,128)(2,1)S(1)} collective-permute-done((bf16[32,1,64]{2,0,1:T(8,128)(2,1)S(1)}, bf16[32,1,64]{2,0,1:T(8,128)(2,1)S(1)}, u32[]{:S(2)}, u32[]{:S(2)}) %collective-permute-start.1) | collective-permute-done | bytes 4128 | tf_op jit(solution)/shard_map/ppermute | solution.py:12
  87.5 0.8 gather_fusion.1
  88.2 6.3 %all-to-all-done.1 = bf16[64,2,4096]{2,1,0:T(2,128)(2,1)} async-done(((bf16[64,2,4096]{2,1,0:T(2,128)(2,1)}), bf16[64,2,4096]{2,1,0:T(2,128)(2,1)}, u32[]{:S(2)}, u32[]{:S(2)}) %all-to-all-start.1) | async-done | bytes 1048608 | tf_op jit(solution)/shard_map/all_to_all | solution.py:53
  94.5 3.8 %reshape.303 = bf16[64,2,64,64]{3,2,1,0:T(8,128)(2,1)S(1)} reshape(bf16[64,2,4096]{2,1,0:T(2,128)(2,1)} %all-to-all-done.1) | data formatting | bytes 2097152
  98.3 1.2 fusion.14
  99.5 2.0 fusion.6
  101.5 0.6 gather_fusion.2
  102.1 5.7 %collective-permute-start.2 = (bf16[32,1,64]{2,0,1:T(8,128)(2,1)S(1)}, bf16[32,1,64]{2,0,1:T(8,128)(2,1)S(1)}, u32[]{:S(2)}, u32[]{:S(2)}) collective-permute-start(bf16[32,1,64]{2,0,1:T(8,128)(2,1)S(1)} %get-tuple-element.10), channel_id=1, source_target_pairs={{0,1},{1,2},{2,3},{3,4},{4,5},{5,6},{6,7},{7,8},{8,9},{9,10},{10,1... | collective-permute-start | bytes 12296 | tf_op jit(solution)/shard_map/ppermute | solution.py:12
  107.7 1.3 collective-permute-start.3
  109.0 0.0 collective-permute-done.2
  109.0 3.1 %collective-permute-done.3 = bf16[32,1,64]{2,0,1:T(8,128)(2,1)S(1)} collective-permute-done((bf16[32,1,64]{2,0,1:T(8,128)(2,1)S(1)}, bf16[32,1,64]{2,0,1:T(8,128)(2,1)S(1)}, u32[]{:S(2)}, u32[]{:S(2)}) %collective-permute-start.3) | collective-permute-done | bytes 4128 | tf_op jit(solution)/shard_map/ppermute | solution.py:12
  112.2 0.8 gather_fusion.3
  112.9 1.2 fusion.12
  114.1 2.0 fusion.4
  116.1 0.6 gather_fusion.4
  116.7 1.9 collective-permute-start.4
  118.6 1.5 collective-permute-start.5
  120.1 0.0 collective-permute-done.4
  120.1 2.9 %collective-permute-done.5 = bf16[32,1,64]{2,0,1:T(8,128)(2,1)S(1)} collective-permute-done((bf16[32,1,64]{2,0,1:T(8,128)(2,1)S(1)}, bf16[32,1,64]{2,0,1:T(8,128)(2,1)S(1)}, u32[]{:S(2)}, u32[]{:S(2)}) %collective-permute-start.5) | collective-permute-done | bytes 4128 | tf_op jit(solution)/shard_map/ppermute | solution.py:12
  123.0 0.8 gather_fusion.5
  123.8 1.2 fusion.10
  125.0 2.0 fusion.2
  127.0 0.6 gather_fusion.6
  127.5 2.1 collective-permute-start.6
  129.6 1.3 collective-permute-start.7
  130.9 0.0 collective-permute-done.6
  130.9 3.1 %collective-permute-done.7 = bf16[32,1,64]{2,0,1:T(8,128)(2,1)S(1)} collective-permute-done((bf16[32,1,64]{2,0,1:T(8,128)(2,1)S(1)}, bf16[32,1,64]{2,0,1:T(8,128)(2,1)S(1)}, u32[]{:S(2)}, u32[]{:S(2)}) %collective-permute-start.7) | collective-permute-done | bytes 4128 | tf_op jit(solution)/shard_map/ppermute | solution.py:12
  134.0 0.8 gather_fusion.7
  134.8 1.2 fusion.8
  136.0 2.0 fusion
  138.0 0.1 fusion.18
  138.1 113.1 %psum.7 = f32[32]{0:T(128)S(1)} all-reduce(f32[32]{0:T(128)S(1)} %get-tuple-element.4), channel_id=1, replica_groups=mesh['grp'=8,'dev'=64] {'grp','dev'}, use_global_device_ids=true, to_apply=%region_5.6 | all-reduce | flops 32 | bytes 256 | tf_op jit(solution)/shard_map/psum | solution.py:90
  251.2 0.5 multiply_sqrt_fusion
  251.8 0.7 reshape.197
  (25 shorter events, 0.2 us)
Async XLA Ops:
  0.6 24.2 %copy-start = (bf16[1,54,64,64]{3,2,1,0:T(8,128)(2,1)S(1)}, bf16[1,54,64,64]{3,2,1,0:T(8,128)(2,1)}, u32[]{:S(2)}) copy-start(bf16[1,54,64,64]{3,2,1,0:T(8,128)(2,1)} %param.8) | copy-start | bytes 1327108
  5.2 32.2 %all-to-all-start = ((s32[64,1,2]{2,1,0:T(1,128)}), s32[64,1,2]{2,1,0:T(1,128)S(1)}, u32[]{:S(2)}, u32[]{:S(2)}) async-start(s32[64,1,2]{2,1,0:T(1,128)} %bitcast.5), calls=%async_computation | async-start | bytes 65536 | tf_op jit(solution)/shard_map/all_to_all | solution.py:54
  27.8 17.2 %copy-start.1 = (f32[1,32,128]{2,1,0:T(8,128)S(1)}, f32[1,32,128]{2,1,0:T(8,128)}, u32[]{:S(2)}) copy-start(f32[1,32,128]{2,1,0:T(8,128)} %param.14) | copy-start | bytes 49156
  27.8 17.3 %copy-start.3 = (s32[1,2]{1,0:T(1,128)S(1)}, s32[1,2]{1,0:T(1,128)}, u32[]{:S(2)}) copy-start(s32[1,2]{1,0:T(1,128)} %param.12) | copy-start | bytes 28
  27.8 22.5 %copy-start.4 = (f32[1,128]{1,0:T(1,128)S(1)}, f32[1,128]{1,0:T(1,128)}, u32[]{:S(2)}) copy-start(f32[1,128]{1,0:T(1,128)} %param.15) | copy-start | bytes 1540
  27.8 23.3 %copy-start.2 = (f32[1,32,128]{2,1,0:T(8,128)S(1)}, f32[1,32,128]{2,1,0:T(8,128)}, u32[]{:S(2)}) copy-start(f32[1,32,128]{2,1,0:T(8,128)} %param.13) | copy-start | bytes 49156
  37.5 57.1 %all-to-all-start.1 = ((bf16[64,2,4096]{2,1,0:T(2,128)(2,1)}), bf16[64,2,4096]{2,1,0:T(2,128)(2,1)}, u32[]{:S(2)}, u32[]{:S(2)}) async-start(bf16[64,2,4096]{2,1,0:T(2,128)(2,1)} %reshape.302), calls=%async_computation.1 | async-start | bytes 2097152 | tf_op jit(solution)/shard_map/all_to_all | solution.py:53
  45.7 32.2 %collective-permute-start = (bf16[32,1,64]{2,0,1:T(8,128)(2,1)S(1)}, bf16[32,1,64]{2,0,1:T(8,128)(2,1)S(1)}, u32[]{:S(2)}, u32[]{:S(2)}) collective-permute-start(bf16[32,1,64]{2,0,1:T(8,128)(2,1)S(1)} %get-tuple-element.12), channel_id=1, source_target_pairs={{0,1},{1,2},{2,3},{3,4},{4,5},{5,6},{6,7},{7,8},{8,9},{9,10},{10,1... | collective-permute-start | bytes 12296 | tf_op jit(solution)/shard_map/ppermute | solution.py:12
  48.5 39.0 %collective-permute-start.1 = (bf16[32,1,64]{2,0,1:T(8,128)(2,1)S(1)}, bf16[32,1,64]{2,0,1:T(8,128)(2,1)S(1)}, u32[]{:S(2)}, u32[]{:S(2)}) collective-permute-start(bf16[32,1,64]{2,0,1:T(8,128)(2,1)S(1)} %get-tuple-element.13), channel_id=1, source_target_pairs={{1,0},{2,1},{3,2},{4,3},{5,4},{6,5},{7,6},{8,7},{9,8},{10,9},{11,1... | collective-permute-start | bytes 12296 | tf_op jit(solution)/shard_map/ppermute | solution.py:12
  102.1 7.0 %collective-permute-start.2 = (bf16[32,1,64]{2,0,1:T(8,128)(2,1)S(1)}, bf16[32,1,64]{2,0,1:T(8,128)(2,1)S(1)}, u32[]{:S(2)}, u32[]{:S(2)}) collective-permute-start(bf16[32,1,64]{2,0,1:T(8,128)(2,1)S(1)} %get-tuple-element.10), channel_id=1, source_target_pairs={{0,1},{1,2},{2,3},{3,4},{4,5},{5,6},{6,7},{7,8},{8,9},{9,10},{10,1... | collective-permute-start | bytes 12296 | tf_op jit(solution)/shard_map/ppermute | solution.py:12
  107.7 4.4 %collective-permute-start.3 = (bf16[32,1,64]{2,0,1:T(8,128)(2,1)S(1)}, bf16[32,1,64]{2,0,1:T(8,128)(2,1)S(1)}, u32[]{:S(2)}, u32[]{:S(2)}) collective-permute-start(bf16[32,1,64]{2,0,1:T(8,128)(2,1)S(1)} %get-tuple-element.11), channel_id=1, source_target_pairs={{1,0},{2,1},{3,2},{4,3},{5,4},{6,5},{7,6},{8,7},{9,8},{10,9},{11,1... | collective-permute-start | bytes 12296 | tf_op jit(solution)/shard_map/ppermute | solution.py:12
  116.7 3.4 %collective-permute-start.4 = (bf16[32,1,64]{2,0,1:T(8,128)(2,1)S(1)}, bf16[32,1,64]{2,0,1:T(8,128)(2,1)S(1)}, u32[]{:S(2)}, u32[]{:S(2)}) collective-permute-start(bf16[32,1,64]{2,0,1:T(8,128)(2,1)S(1)} %get-tuple-element.8), channel_id=1, source_target_pairs={{0,1},{1,2},{2,3},{3,4},{4,5},{5,6},{6,7},{7,8},{8,9},{9,10},{10,1... | collective-permute-start | bytes 12296 | tf_op jit(solution)/shard_map/ppermute | solution.py:12
  118.6 4.4 %collective-permute-start.5 = (bf16[32,1,64]{2,0,1:T(8,128)(2,1)S(1)}, bf16[32,1,64]{2,0,1:T(8,128)(2,1)S(1)}, u32[]{:S(2)}, u32[]{:S(2)}) collective-permute-start(bf16[32,1,64]{2,0,1:T(8,128)(2,1)S(1)} %get-tuple-element.9), channel_id=1, source_target_pairs={{1,0},{2,1},{3,2},{4,3},{5,4},{6,5},{7,6},{8,7},{9,8},{10,9},{11,1... | collective-permute-start | bytes 12296 | tf_op jit(solution)/shard_map/ppermute | solution.py:12
  127.5 3.4 %collective-permute-start.6 = (bf16[32,1,64]{2,0,1:T(8,128)(2,1)S(1)}, bf16[32,1,64]{2,0,1:T(8,128)(2,1)S(1)}, u32[]{:S(2)}, u32[]{:S(2)}) collective-permute-start(bf16[32,1,64]{2,0,1:T(8,128)(2,1)S(1)} %get-tuple-element.6), channel_id=1, source_target_pairs={{0,1},{1,2},{2,3},{3,4},{4,5},{5,6},{6,7},{7,8},{8,9},{9,10},{10,1... | collective-permute-start | bytes 12296 | tf_op jit(solution)/shard_map/ppermute | solution.py:12
  129.6 4.4 %collective-permute-start.7 = (bf16[32,1,64]{2,0,1:T(8,128)(2,1)S(1)}, bf16[32,1,64]{2,0,1:T(8,128)(2,1)S(1)}, u32[]{:S(2)}, u32[]{:S(2)}) collective-permute-start(bf16[32,1,64]{2,0,1:T(8,128)(2,1)S(1)} %get-tuple-element.7), channel_id=1, source_target_pairs={{1,0},{2,1},{3,2},{4,3},{5,4},{6,5},{7,6},{8,7},{9,8},{10,9},{11,1... | collective-permute-start | bytes 12296 | tf_op jit(solution)/shard_map/ppermute | solution.py:12
where the time goes:
time: 253 us; the launch traced here: 252 us
  blocking collectives  113 us (45%)
  waiting for transfers between devices  57.4 us (23%)
  starting transfers between devices  44.4 us (18%)
  local copies, waits for them, and re-layouts  18.6 us (7%)
  matrix products  12.6 us (5%)
  other arithmetic  5.28 us (2%)
    psum x1, blocking collectives, shards(): lax.psum(jnp.sum(residual * residual, axis=(1, 2)), ('grp', 'dev'))  113 us
    ppermute x8, waiting for transfers between devices, from_behind(): lax.ppermute(value, axis, [(source, source + steps) for source in range(i...  43.8 us
    all_to_all x1, starting transfers between devices, shards(): lax.all_to_all(sent_place, 'dev', split_axis=0, concat_axis=0, tiled=True)  19.1 us
    ppermute x8, starting transfers between devices, from_behind(): lax.ppermute(value, axis, [(source, source + steps) for source in range(i...  17.8 us
    dot_general x4, matrix products, apply_op(): jnp.einsum('sri,sb->rbi', products, row_onehot, precision=lax.Precision.H...  7.88 us
    all_to_all x1, starting transfers between devices, shards(): lax.all_to_all(sent_tiles, 'dev', split_axis=0, concat_axis=0, tiled=True)  7.48 us
    all_to_all x1, waiting for transfers between devices, shards(): lax.all_to_all(sent_place, 'dev', split_axis=0, concat_axis=0, tiled=True)  7.36 us
    unnamed x13, local copies, waits for them, and re-layouts  6.61 us
  transfers between devices with their start and end apart: 10, of which 7 were waited for; matrix products, arithmetic and copies ran while one was open for 4% of the time, Pallas kernels for 0%

commit v1 on v0

v1 whole, which is shorter than its diff:
```python
import functools

import jax
import jax.numpy as jnp
from jax import lax
from jax.experimental import pallas as pl
from jax.experimental.pallas import tpu as pltpu
from jax.sharding import PartitionSpec as P

STEPS = 3
NZ = 16
CH = 4
MESH = pl.DeviceIdType.MESH


def kernel(
    ng, nx, nz,
    owner_s, rows_s, cols_s, ghost_s, tiles_hbm, rhs_ref, start_ref, diag_ref,
    out_ref, rms_ref,
    tiles_v, tab_v, tab_s, plc_send, plc, xsend, xbuf, rsend, rrecv, wmat,
    gsend, grecv, red_g, red_x, red_z,
    tile_sem, tab_sem, plc_ss, plc_rs, x_ss, x_rs, r_ss, r_rs, g_ss, g_rs,
    red_g_ss, red_g_rs, red_x_ss, red_x_rs, red_z_ss, red_z_rs,
):
    half = nz // 2
    ndev = nx * nz
    tcount = tiles_v.shape[0]
    dev = lax.axis_index("dev")
    grp = lax.axis_index("grp")
    x = lax.div(dev, nz)
    z = lax.rem(dev, nz)

    def x_peer(j):
        return {"dev": lax.rem(x + j, nx) * nz + z}

    def z_peer(k):
        return {"dev": x * nz + lax.rem(z + k, nz)}

    def g_peer(k):
        return {"grp": lax.rem(grp + k, ng)}

    upper = {"dev": lax.rem(dev + 1, ndev)}
    lower = {"dev": lax.rem(dev + ndev - 1, ndev)}

    tile_copy = pltpu.make_async_copy(tiles_hbm.at[0], tiles_v, tile_sem)
    tile_copy.start()

    barrier = pltpu.get_barrier_semaphore()
    peers = [x_peer(j) for j in range(1, nx)] + [z_peer(k) for k in range(1, nz)]
    peers += [g_peer(k) for k in range(1, ng)] + [upper, lower]
    for peer in peers:
        pl.semaphore_signal(barrier, inc=1, device_id=peer, device_id_type=MESH)

    lane = lax.broadcasted_iota(jnp.int32, (1, 128), 1)
    none = jnp.full((1, 128), -1, jnp.int32)

    def find(t, held):
        i0, i1, p0, p1 = held
        hit = lane == owner_s[0, t]
        place = rows_s[0, t] * 4 + cols_s[0, t]
        first = jnp.logical_and(hit, i0 < 0)
        second = jnp.logical_and(hit, i0 >= 0)
        return (
            jnp.where(first, t, i0), jnp.where(second, t, i1),
            jnp.where(first, place, p0), jnp.where(second, place, p1),
        )

    i0, i1, p0, p1 = lax.fori_loop(0, tcount, find, (none,) * 4, unroll=True)
    tab_v[0:1, :] = jnp.maximum(i0, 0)
    tab_v[1:2, :] = jnp.maximum(i1, 0)
    tab_v[2:3, :] = p0
    tab_v[3:4, :] = p1
    tab_copy = pltpu.make_async_copy(tab_v, tab_s, tab_sem)
    tab_copy.start()

    wide = lax.broadcasted_iota(jnp.int32, (rhs_ref.shape[1], 128), 1)
    left = wide < 64
    stay = jnp.where(left, ghost_s[0, 1], 1 - ghost_s[0, 0]) == 0

    def ghost_copies(n):
        return [
            pltpu.make_async_remote_copy(
                src_ref=gsend.at[n], dst_ref=grecv.at[n, way],
                send_sem=g_ss.at[n, way], recv_sem=g_rs.at[n, way],
                device_id=peer, device_id_type=MESH,
            )
            for way, peer in enumerate((upper, lower))
        ]

    def send_ghosts(n, vec):
        gsend[n] = jnp.where(stay, vec, pltpu.roll(vec, 64, 1)).astype(jnp.bfloat16)
        for copy in ghost_copies(n):
            copy.start()

    pl.semaphore_wait(barrier, len(peers))

    start = start_ref[0]
    send_ghosts(0, start)

    tab_copy.wait()

    def owner_of(j, fam, m):
        step = half - m if fam == 0 else m + nz - (half - 1)
        return lax.rem(x + j, nx) * nz + lax.rem(z + step, nz)

    def set_places(m, _):
        for j in range(nx):
            for fam in range(2):
                o = owner_of(j, fam, m)
                row = jnp.where(lane < 64, tab_s[2, o], tab_s[3, o])
                if j == 0:
                    plc[0, pl.ds(m * 2 + fam, 1), :] = row
                else:
                    plc_send[j, pl.ds(m * 2 + fam, 1), :] = row
        return 0

    lax.fori_loop(0, half, set_places, 0)

    def plc_copy(j):
        return pltpu.make_async_remote_copy(
            src_ref=plc_send.at[j], dst_ref=plc.at[j],
            send_sem=plc_ss.at[j - 1], recv_sem=plc_rs.at[j - 1],
            device_id=x_peer(j), device_id_type=MESH,
        )

    for j in range(1, nx):
        plc_copy(j).start()

    def x_copy(j, m):
        return pltpu.make_async_remote_copy(
            src_ref=xsend.at[j, m], dst_ref=xbuf.at[j, m],
            send_sem=x_ss.at[j - 1, m], recv_sem=x_rs.at[j - 1, m],
            device_id=x_peer(j), device_id_type=MESH,
        )

    tile_copy.wait()

    def pack(m, _):
        for j in list(range(1, nx)) + [0]:
            for fam in range(2):
                o = owner_of(j, fam, m)
                pair = jnp.concatenate([tiles_v[tab_s[0, o]], tiles_v[tab_s[1, o]]], axis=1)
                if j == 0:
                    xbuf[0, m, fam] = pair
                else:
                    xsend[j, m, fam] = pair
            if j:
                x_copy(j, m).start()
        return 0

    lax.fori_loop(0, half, pack, 0)

    for j in range(1, nx):
        plc_copy(j).wait_recv()

    right_half = (lane >= 64).astype(jnp.int32)

    def dense(fam, m):
        acc = [jnp.zeros((64, 128), jnp.float32) for _ in range(CH)]
        for j in range(nx):
            pair = xbuf[j, m, fam].astype(jnp.float32)
            swapped = pltpu.roll(pair, 64, 1)
            row = plc[j, pl.ds(m * 2 + fam, 1), :]
            row_swapped = pltpu.roll(row, 64, 1)
            for c in range(CH):
                target = (c // 2) * 4 + (c % 2) * 2 + right_half
                acc[c] += jnp.where(row == target, pair, 0.0)
                acc[c] += jnp.where(row_swapped == target, swapped, 0.0)
        for c in range(CH):
            rsend[fam, m, c] = acc[c]

    def prepare(m):
        for j in range(1, nx):
            x_copy(j, m).wait_recv()
        dense(0, m)
        dense(1, m)

    def ring_copy(way, s, c):
        return pltpu.make_async_remote_copy(
            src_ref=rsend.at[way, s, c], dst_ref=rrecv.at[way, s, c],
            send_sem=r_ss.at[way, s, c], recv_sem=r_rs.at[way, s, c],
            device_id=z_peer(1 if way == 0 else nz - 1), device_id_type=MESH,
        )

    def forward(way, s, c):
        ring_copy(way, s - 1, c).wait_recv()
        rsend[way, s, c] = rsend[way, s, c] + rrecv[way, s - 1, c]
        ring_copy(way, s, c).start()

    prepare(0)
    for c in range(CH):
        for way in range(2):
            ring_copy(way, 0, c).start()
    prepare(1)

    def ring(s, _):
        for c in range(CH):
            for way in range(2):
                forward(way, s, c)
        prepare(s + 1)
        return 0

    lax.fori_loop(1, half - 1, ring, 0)
    for c in range(CH):
        forward(0, half - 1, c)
    for c in range(CH):
        ring_copy(1, half - 2, c).wait_recv()
        ring_copy(0, half - 1, c).wait_recv()
        total = rsend[1, half - 1, c] + rrecv[1, half - 2, c] + rrecv[0, half - 1, c]
        high = total.astype(jnp.bfloat16)
        low = (total - high.astype(jnp.float32)).astype(jnp.bfloat16)
        r, cp = (c // 2) * 64, (c % 2) * 128
        wmat[r:r + 64, cp:cp + 128] = high
        wmat[128 + r:192 + r, cp:cp + 128] = low

    diag = diag_ref[...]
    inverse = 1.0 / diag
    from_lower = jnp.logical_and(left, dev > 0)
    from_upper = jnp.logical_and(jnp.logical_not(left), dev < ndev - 1)

    def apply_op(n, vec):
        for copy in ghost_copies(n):
            copy.wait_recv()
        ghosts = jnp.where(from_lower, grecv[n, 0].astype(jnp.float32), 0.0)
        ghosts = jnp.where(from_upper, grecv[n, 1].astype(jnp.float32), ghosts)
        extended = jnp.concatenate([vec, ghosts], axis=1).astype(jnp.bfloat16)
        both = lax.dot_general(
            extended, wmat[...], (((1,), (1,)), ((), ())), preferred_element_type=jnp.float32
        )
        return diag * vec + (both[:, :128] + both[:, 128:])

    lmax = 2.0
    lmin = 0.2
    theta = (lmax + lmin) / 2.0
    delta = (lmax - lmin) / 2.0
    sigma = theta / delta
    rho = 1.0 / sigma
    iterate = start
    residual = rhs_ref[0] - apply_op(0, start)
    direction = residual * (inverse * (1.0 / theta))
    for step in range(STEPS):
        send_ghosts(step + 1, direction)
        iterate = iterate + direction
        residual = residual - apply_op(step + 1, direction)
        if step + 1 < STEPS:
            rho_new = 1.0 / (2.0 * sigma - rho)
            direction = (rho_new * rho) * direction + (2.0 * rho_new / delta) * residual * inverse
            rho = rho_new
    out_ref[0] = iterate

    width = rhs_ref.shape[1]
    squares = jnp.sum((residual * residual).T, axis=0, keepdims=True)
    part = jnp.concatenate([squares, jnp.zeros((1, 128 - width), jnp.float32)], axis=1)
    sent = []
    for buf, ss, rs, here, count, peer in (
        (red_g, red_g_ss, red_g_rs, grp, ng, g_peer),
        (red_x, red_x_ss, red_x_rs, x, nx, x_peer),
        (red_z, red_z_ss, red_z_rs, z, nz, z_peer),
    ):
        buf[here] = part
        copies = [
            pltpu.make_async_remote_copy(
                src_ref=buf.at[here], dst_ref=buf.at[here],
                send_sem=ss.at[k - 1], recv_sem=rs.at[k - 1],
                device_id=peer(k), device_id_type=MESH,
            )
            for k in range(1, count)
        ]
        for copy in copies:
            copy.start()
        for k in range(1, count):
            other = lax.rem(here + count - k, count)
            pltpu.make_async_remote_copy(
                src_ref=buf.at[here], dst_ref=buf.at[other],
                send_sem=ss.at[k - 1], recv_sem=rs.at[k - 1],
                device_id=peer(k), device_id_type=MESH,
            ).wait_recv()
        part = buf[0]
        for k in range(1, count):
            part = part + buf[k]
        sent += copies
    rms_ref[...] = jnp.sqrt(part * (1.0 / (ng * ndev * 128)))[:, :width]

    for copy in sent:
        copy.wait_send()
    for n in range(STEPS + 1):
        for copy in ghost_copies(n):
            copy.wait_send()
    for j in range(1, nx):
        plc_copy(j).wait_send()

    def drain(s, _):
        for j in range(1, nx):
            x_copy(j, s).wait_send()
        for c in range(CH):
            ring_copy(0, s, c).wait_send()
        return 0

    lax.fori_loop(0, half, drain, 0)

    def drain_down(s, _):
        for c in range(CH):
            ring_copy(1, s, c).wait_send()
        return 0

    lax.fori_loop(0, half - 1, drain_down, 0)


def shards(ng, nx, nz, tiles, owner, tile_rows, tile_cols, ghost_rows, rhs, start, diag):
    tcount, block = tiles.shape[1], tiles.shape[2]
    width = rhs.shape[1]
    half = nz // 2
    f32, bf16, i32 = jnp.float32, jnp.bfloat16, jnp.int32
    dma = pltpu.SemaphoreType.DMA
    smem = pl.BlockSpec(memory_space=pltpu.SMEM)
    vmem = pl.BlockSpec(memory_space=pltpu.VMEM)
    smoothed, rms = pl.pallas_call(
        functools.partial(kernel, ng, nx, nz),
        out_shape=(
            jax.ShapeDtypeStruct((1, width, 128), f32),
            jax.ShapeDtypeStruct((1, width), f32),
        ),
        in_specs=[smem] * 4 + [pl.BlockSpec(memory_space=pl.ANY)] + [vmem] * 3,
        out_specs=(vmem, vmem),
        scratch_shapes=[
            pltpu.VMEM((tcount, block, block), bf16),
            pltpu.VMEM((8, 128), i32),
            pltpu.SMEM((8, 128), i32),
            pltpu.VMEM((nx, nz, 128), i32),
            pltpu.VMEM((nx, nz, 128), i32),
            pltpu.VMEM((nx, half, 2, 64, 128), bf16),
            pltpu.VMEM((nx, half, 2, 64, 128), bf16),
            pltpu.VMEM((2, half, CH, 64, 128), f32),
            pltpu.VMEM((2, half, CH, 64, 128), f32),
            pltpu.VMEM((256, 256), bf16),
            pltpu.VMEM((STEPS + 1, width, 128), bf16),
            pltpu.VMEM((STEPS + 1, 2, width, 128), bf16),
            pltpu.VMEM((ng, 1, 128), f32),
            pltpu.VMEM((nx, 1, 128), f32),
            pltpu.VMEM((nz, 1, 128), f32),
            dma,
            dma,
            dma((nx - 1,)),
            dma((nx - 1,)),
            dma((nx - 1, half)),
            dma((nx - 1, half)),
            dma((2, half, CH)),
            dma((2, half, CH)),
            dma((STEPS + 1, 2)),
            dma((STEPS + 1, 2)),
            dma((ng - 1,)),
            dma((ng - 1,)),
            dma((nx - 1,)),
            dma((nx - 1,)),
            dma((nz - 1,)),
            dma((nz - 1,)),
        ],
        compiler_params=pltpu.CompilerParams(
            collective_id=0, has_side_effects=True, vmem_limit_bytes=32 * 1024 * 1024
        ),
    )(owner.reshape(1, tcount), tile_rows, tile_cols, ghost_rows, tiles, rhs, start, diag)
    return smoothed, rms.reshape(width)


def solution(mesh):
    ng = mesh.shape["grp"]
    nx = mesh.shape["dev"] // NZ
    return jax.shard_map(
        functools.partial(shards, ng, nx, NZ),
        mesh=mesh,
        in_specs=(
            P("grp", "dev", None, None),
            P("grp", "dev", None),
            P("grp", "dev"),
            P("grp", "dev"),
            P("grp", "dev"),
            P("grp", None, "dev"),
            P("grp", None, "dev"),
            P("grp", "dev"),
        ),
        out_specs=(P("grp", None, "dev"), P()),
        check_vma=False,
    )
```

time: 253 us -> 84.1 us (0.33)
  blocking collectives: 113 us -> 0 us
  Pallas kernels: 0 us -> 77.2 us
  waiting for transfers between devices: 57.4 us -> 0 us
  starting transfers between devices: 44.4 us -> 0 us
  local copies, waits for them, and re-layouts: 18.6 us -> 5.69 us
  matrix products: 12.6 us -> 0 us
  other arithmetic: 5.28 us -> 0 us
    psum x1 -> x0, blocking collectives: 113 us -> none  [shards(): lax.psum(jnp.sum(residual * residual, axis=(1, 2)), ('grp', 'dev'))]
    pallas_call x0 -> x1, Pallas kernels: none -> 77.2 us  [shards(): pl.pallas_call(functools.partial(kernel, ng, nx, nz), out_shape=(jax.Shap...]
    ppermute x8 -> x0, waiting for transfers between devices: 43.8 us -> none  [from_behind(): lax.ppermute(value, axis, [(source, source + steps) for source in range(i...]
    all_to_all x2 -> x0, starting transfers between devices: 26.6 us -> none  [the longest x1 19.1 us: shards(): lax.all_to_all(sent_place, 'dev', split_axis=0, concat_axis=0, tiled=True)]
    ppermute x8 -> x0, starting transfers between devices: 17.8 us -> none  [from_behind(): lax.ppermute(value, axis, [(source, source + steps) for source in range(i...]
    all_to_all x2 -> x0, waiting for transfers between devices: 13.6 us -> none  [the longest x1 7.36 us: shards(): lax.all_to_all(sent_place, 'dev', split_axis=0, concat_axis=0, tiled=True)]
    dot_general x8 -> x0, matrix products: 12.6 us -> none  [the longest x4 7.88 us: apply_op(): jnp.einsum('sri,sb->rbi', products, row_onehot, precision=lax.Precision.H...]
    gather x8 -> x0, local copies, waits for them, and re-layouts: 5.28 us -> none  [the longest x4 3.05 us: apply_op(): picked = extended[:, dest_cols, :]]
  transfers between devices with their start and end apart: 10 -> 0, of which waited for: 7 -> 0; matrix products, arithmetic and copies ran while one was open for 4% -> 0% of each run, Pallas kernels for 0% -> 0%
where the time goes in v1:
time: 84.1 us; the launch traced here: 83.5 us
  Pallas kernels  77.2 us (92%)
  local copies, waits for them, and re-layouts  5.69 us (7%)
    pallas_call x1, Pallas kernels, shards(): pl.pallas_call(functools.partial(kernel, ng, nx, nz), out_shape=(jax.Shap...  77.2 us
    unnamed x18, local copies, waits for them, and re-layouts  5.69 us

profile of v1, /device:TPU:1, one launch (start us, length us, event | category | flops | bytes accessed | tf_op | source)
XLA Modules:
  0.0 83.5 jit_solution(1718278235182921160)
XLA Ops:
  0.6 0.0 copy-start.5
  0.6 0.0 copy-start.4
  0.7 0.0 copy-start.3
  0.7 0.6 copy-done.5
  1.3 0.0 copy-done.4
  1.3 0.0 copy-done.3
  1.3 0.0 copy-start
  1.3 1.2 %copy-done = bf16[1,54,64,64]{3,2,1,0:T(8,128)(2,1)S(1)} copy-done((bf16[1,54,64,64]{3,2,1,0:T(8,128)(2,1)S(1)}, bf16[1,54,64,64]{3,2,1,0:T(8,128)(2,1)}, u32[]{:S(2)}) %copy-start) | copy-done | bytes 442392
  2.5 0.0 copy-start.1
  2.5 0.7 copy-done.1
  3.2 0.0 copy-start.2
  3.2 0.7 copy-done.2
  3.9 0.0 copy-start.6
  3.9 0.7 copy-done.6
  4.6 0.0 copy-start.7
  4.6 0.7 copy-done.7
  5.2 77.2 %shard_map.95 = (f32[1,32,128]{2,1,0:T(8,128)S(1)}, f32[1,32]{1,0:T(1,128)S(1)}) custom-call(s32[1,54]{1,0:T(1,128)S(1)} %bitcast.2, s32[1,54]{1,0:T(1,128)S(1)} %copy-done.4, s32[1,54]{1,0:T(1,128)S(1)} %copy-done.5, s32[1,2]{1,0:T(1,128)S(1)} %copy-done.6, bf16[1,54,64,64]{3,2,1,0:T(8,128)(2,1)S(1)} %copy-done, f32[1,32,128]{2,1,0:T(8,128)S(1)} %copy-done.1, ...), custom_call_target="tpu_custom_call" | custom-call | tf_op jit(solution)/shard_map/pallas_call | solution.py:317
  82.4 0.6 copy.12
  83.0 0.5 copy.13
Async XLA Ops:
  0.6 0.7 copy-start.5
  0.6 0.7 copy-start.4
  0.7 0.7 copy-start.3
  1.3 1.2 %copy-start = (bf16[1,54,64,64]{3,2,1,0:T(8,128)(2,1)S(1)}, bf16[1,54,64,64]{3,2,1,0:T(8,128)(2,1)}, u32[]{:S(2)}) copy-start(bf16[1,54,64,64]{3,2,1,0:T(8,128)(2,1)} %tiles_hbm.1) | copy-start | bytes 1327108
  2.5 0.7 copy-start.1
  3.2 0.7 copy-start.2
  3.9 0.7 copy-start.6
  4.6 0.7 copy-start.7

commit v2 on v1

v2 whole, which is shorter than its diff:
```python
import functools

import jax
import jax.numpy as jnp
from jax import lax
from jax.experimental import pallas as pl
from jax.experimental.pallas import tpu as pltpu
from jax.sharding import PartitionSpec as P

STEPS = 3
NZ = 16
CH = 4
MESH = pl.DeviceIdType.MESH


def kernel(
    ng, nx, nz,
    owner_h, rows_h, cols_h, ghost_h, tiles_h, rhs_h, start_h, diag_h,
    out_ref, rms_ref,
    owner_s, rows_s, cols_s, ghost_s, tiles_v, rhs_v, start_v, diag_v,
    tab_v, tab_s, po_send, po, pl_send, pl_recv, pq,
    osend, xown, lsend, lrecv, xleaf, dmat, qsend, qrecv, ssend, srecv, wmat,
    gsend, grecv, red_g, red_x, red_z,
    in_sem, tab_sem, po_ss, po_rs, pl_ss, pl_rs, pq_ss, pq_rs,
    o_ss, o_rs, l_ss, l_rs, y_ss, y_rs, q_ss, q_rs, s_ss, s_rs, g_ss, g_rs,
    red_g_ss, red_g_rs, red_x_ss, red_x_rs, red_z_ss, red_z_rs,
):
    half = nz // 2
    nk = half // 2
    ndev = nx * nz
    tcount = tiles_v.shape[0]
    width = rhs_v.shape[0]
    dev = lax.axis_index("dev")
    grp = lax.axis_index("grp")
    x = lax.div(dev, nz)
    z = lax.rem(dev, nz)

    def x_peer(j):
        return {"dev": lax.rem(x + j, nx) * nz + z}

    def z_peer(k):
        return {"dev": x * nz + lax.rem(z + k + nz, nz)}

    def g_peer(k):
        return {"grp": lax.rem(grp + k, ng)}

    upper = {"dev": lax.rem(dev + 1, ndev)}
    lower = {"dev": lax.rem(dev + ndev - 1, ndev)}

    fetches = [
        pltpu.make_async_copy(src, dst, in_sem.at[n])
        for n, (src, dst) in enumerate((
            (owner_h, owner_s), (rows_h, rows_s), (cols_h, cols_s), (ghost_h, ghost_s),
            (tiles_h.at[0], tiles_v), (start_h.at[0], start_v), (rhs_h.at[0], rhs_v),
            (diag_h, diag_v),
        ))
    ]
    for fetch in fetches:
        fetch.start()

    barrier = pltpu.get_barrier_semaphore()
    peers = [upper, lower, z_peer(1), z_peer(-1), z_peer(2), z_peer(-2)]
    peers += [x_peer(j) for j in range(1, nx)] + [g_peer(k) for k in range(1, ng)]
    for peer in peers:
        pl.semaphore_signal(barrier, inc=1, device_id=peer, device_id_type=MESH)

    lane = lax.broadcasted_iota(jnp.int32, (1, 128), 1)
    none = jnp.full((1, 128), -1, jnp.int32)
    for fetch in fetches[:4]:
        fetch.wait()

    def find(t, held):
        i0, i1, p0, p1 = held
        hit = lane == owner_s[0, t]
        place = rows_s[0, t] * 4 + cols_s[0, t]
        first = jnp.logical_and(hit, i0 < 0)
        second = jnp.logical_and(hit, i0 >= 0)
        return (
            jnp.where(first, t, i0), jnp.where(second, t, i1),
            jnp.where(first, place, p0), jnp.where(second, place, p1),
        )

    i0, i1, p0, p1 = lax.fori_loop(0, tcount, find, (none,) * 4, unroll=True)
    tab_v[0:1, :] = jnp.maximum(i0, 0)
    tab_v[1:2, :] = jnp.maximum(i1, 0)
    tab_v[2:3, :] = p0
    tab_v[3:4, :] = p1
    tab_copy = pltpu.make_async_copy(tab_v, tab_s, tab_sem)
    tab_copy.start()

    wide = lax.broadcasted_iota(jnp.int32, (width, 128), 1)
    left = wide < 64
    stay = jnp.where(left, ghost_s[0, 1], 1 - ghost_s[0, 0]) == 0

    def ghost_copies(n):
        return [
            pltpu.make_async_remote_copy(
                src_ref=gsend.at[n], dst_ref=grecv.at[n, way],
                send_sem=g_ss.at[n, way], recv_sem=g_rs.at[n, way],
                device_id=peer, device_id_type=MESH,
            )
            for way, peer in enumerate((upper, lower))
        ]

    def send_ghosts(n, vec):
        gsend[n] = jnp.where(stay, vec, pltpu.roll(vec, 64, 1)).astype(jnp.bfloat16)
        for copy in ghost_copies(n):
            copy.start()

    def remote(src, dst, ss, rs, peer):
        return pltpu.make_async_remote_copy(
            src_ref=src, dst_ref=dst, send_sem=ss, recv_sem=rs,
            device_id=peer, device_id_type=MESH,
        )

    def owner_of(j, step):
        return lax.rem(x + j, nx) * nz + lax.rem(z + step + nz, nz)

    def own_step(fam, k):
        if fam == 0:
            return half - 2 * k
        return 0 if k == 0 else 2 * k - half

    def leaf_step(way, k):
        return half - 1 - 2 * k if way == 0 else 2 * k + 1 - half

    def pair(o):
        return jnp.concatenate([tiles_v[tab_s[0, o]], tiles_v[tab_s[1, o]]], axis=1)

    def place(o):
        return jnp.where(lane < 64, tab_s[2, o], tab_s[3, o])

    def po_copy(j):
        return remote(po_send.at[j], po.at[j], po_ss.at[j - 1], po_rs.at[j - 1], x_peer(j))

    def pl_copy(way):
        return remote(
            pl_send.at[way], pl_recv.at[way], pl_ss.at[way], pl_rs.at[way],
            z_peer(1 if way == 0 else -1),
        )

    def pq_copy(j):
        return remote(pl_recv.at[:, j], pq.at[j], pq_ss.at[j - 1], pq_rs.at[j - 1], x_peer(j))

    def own_copy(j, k, fam):
        return remote(
            osend.at[j, k, fam], xown.at[j, k, fam],
            o_ss.at[j - 1, k, fam], o_rs.at[j - 1, k, fam], x_peer(j),
        )

    def leaf_copy(way, k):
        return remote(
            lsend.at[way, k], lrecv.at[k, way], l_ss.at[way, k], l_rs.at[way, k],
            z_peer(1 if way == 0 else -1),
        )

    def relay_copy(j, k):
        return remote(
            lrecv.at[k, :, j], xleaf.at[j, k], y_ss.at[j - 1, k], y_rs.at[j - 1, k], x_peer(j)
        )

    def pack_own(k, fam):
        for j in list(range(1, nx)) + [0]:
            both = pair(owner_of(j, own_step(fam, k)))
            if j:
                osend[j, k, fam] = both
                own_copy(j, k, fam).start()
            else:
                xown[0, k, fam] = both

    def pack_leaf(k):
        for way in range(2):
            for j in range(nx):
                lsend[way, k, j] = pair(owner_of(j, leaf_step(way, k)))
            leaf_copy(way, k).start()

    def relay(k):
        for way in range(2):
            leaf_copy(way, k).wait_recv()
        if k == 0:
            for way in range(2):
                pl_copy(way).wait_recv()
            for j in range(1, nx):
                pq_copy(j).start()
            pq[0] = pl_recv[:, 0]
        for j in range(1, nx):
            relay_copy(j, k).start()
        xleaf[0, k] = lrecv[k, :, 0]

    tab_copy.wait()
    fetches[4].wait()
    fetches[5].wait()
    start = start_v[...]
    for j in range(nx):
        for k in range(nk):
            for fam in range(2):
                row = place(owner_of(j, own_step(fam, k)))
                n = k * 2 + fam
                if j:
                    po_send[j, n:n + 1, :] = row
                else:
                    po[0, n:n + 1, :] = row
                pl_send[fam, j, k:k + 1, :] = place(owner_of(j, leaf_step(fam, k)))

    pl.semaphore_wait(barrier, len(peers))
    for j in range(1, nx):
        po_copy(j).start()
    pack_own(0, 0)
    for way in range(2):
        pl_copy(way).start()
    pack_leaf(0)
    for k in range(1, nk):
        pack_own(k, 0)
        pack_own(k, 1)
        pack_leaf(k)
    pack_own(0, 1)
    send_ghosts(0, start)

    right_half = (lane >= 64).astype(jnp.int32)

    def add_pair(acc, both, row):
        both = both.astype(jnp.float32)
        swapped = pltpu.roll(both, 64, 1)
        row_swapped = pltpu.roll(row, 64, 1)
        out = []
        for c in range(CH):
            target = (c // 2) * 4 + (c % 2) * 2 + right_half
            value = acc[c] + jnp.where(row == target, both, 0.0)
            out.append(value + jnp.where(row_swapped == target, swapped, 0.0))
        return tuple(out)

    def dense(n, own, leaves):
        k, fam = own
        for j in range(1, nx):
            own_copy(j, k, fam).wait_recv()

        def column(j, acc):
            acc = add_pair(acc, xown[j, k, fam], po[j, k * 2 + fam:k * 2 + fam + 1, :])
            for way, kk in leaves:
                acc = add_pair(acc, xleaf[j, kk, way], pq[j, way, kk:kk + 1, :])
            return acc

        acc = lax.fori_loop(
            0, nx, column, tuple(jnp.zeros((64, 128), jnp.float32) for _ in range(CH))
        )
        for c in range(CH):
            dmat[n, c] = acc[c]

    def chain_copies(way, s, h):
        peer = z_peer(2 if way == 0 else -2)
        return (
            remote(
                ssend.at[way, s, h], srecv.at[way, s, h], s_ss.at[way, s, h],
                s_rs.at[way, s, h], peer,
            ),
            remote(
                qsend.at[way, s, h], qrecv.at[way, s, h], q_ss.at[way, s, h],
                q_rs.at[way, s, h], peer,
            ),
        )

    def send_half(way, s, h, values):
        for cp in range(2):
            most = jnp.maximum(jnp.max(jnp.abs(values[cp]), axis=0, keepdims=True), 1e-30)
            scaled = jnp.round(values[cp] * (32767.0 / most))
            qsend[way, s, h, cp] = scaled.astype(jnp.int32).astype(jnp.int16)
            ssend[way, s, h, cp:cp + 1, :] = most * (1.0 / 32767.0)
        for copy in chain_copies(way, s, h):
            copy.start()

    def arrived(way, s, h, cp):
        whole = qrecv[way, s, h, cp].astype(jnp.int32).astype(jnp.float32)
        return whole * srecv[way, s, h, cp:cp + 1, :]

    def halves(way, s):
        return (way,) if s == 0 else (0, 1)

    for j in range(1, nx):
        po_copy(j).wait_recv()
    dense(0, (0, 0), ())
    for way in range(2):
        send_half(way, 0, way, [dmat[0, way * 2 + cp] for cp in range(2)])
    for k in range(nk):
        relay(k)
        if k == 0:
            for j in range(1, nx):
                pq_copy(j).wait_recv()
        for j in range(1, nx):
            relay_copy(j, k).wait_recv()
        s = k + 1
        if s < nk:
            for way in range(2):
                dense(way, (s, way), ((way, k),))
            for h in range(2):
                for way in range(2):
                    values = [dmat[way, h * 2 + cp] for cp in range(2)]
                    if h in halves(way, k):
                        for copy in chain_copies(way, k, h):
                            copy.wait_recv()
                        values = [values[cp] + arrived(way, k, h, cp) for cp in range(2)]
                    send_half(way, s, h, values)
    dense(0, (0, 1), ((0, nk - 1), (1, nk - 1)))
    for h in range(2):
        values = [dmat[0, h * 2 + cp] for cp in range(2)]
        for way in range(2):
            if h in halves(way, nk - 1):
                for copy in chain_copies(way, nk - 1, h):
                    copy.wait_recv()
                values = [values[cp] + arrived(way, nk - 1, h, cp) for cp in range(2)]
        for cp in range(2):
            high = values[cp].astype(jnp.bfloat16)
            low = (values[cp] - high.astype(jnp.float32)).astype(jnp.bfloat16)
            wmat[h * 64:h * 64 + 64, cp * 128:cp * 128 + 128] = high
            wmat[128 + h * 64:192 + h * 64, cp * 128:cp * 128 + 128] = low

    fetches[6].wait()
    fetches[7].wait()
    diag = diag_v[...]
    inverse = 1.0 / diag
    from_lower = jnp.logical_and(left, dev > 0)
    from_upper = jnp.logical_and(jnp.logical_not(left), dev < ndev - 1)

    def product(vec, columns):
        both = lax.dot_general(
            vec.astype(jnp.bfloat16), wmat[:, columns:columns + 128],
            (((1,), (1,)), ((), ())), preferred_element_type=jnp.float32,
        )
        return both[:, :128] + both[:, 128:]

    def own_part(vec):
        return diag * vec + product(vec, 0)

    def ghost_part(n):
        for copy in ghost_copies(n):
            copy.wait_recv()
        ghosts = jnp.where(from_lower, grecv[n, 0].astype(jnp.float32), 0.0)
        ghosts = jnp.where(from_upper, grecv[n, 1].astype(jnp.float32), ghosts)
        return product(ghosts, 128)

    lmax = 2.0
    lmin = 0.2
    theta = (lmax + lmin) / 2.0
    delta = (lmax - lmin) / 2.0
    sigma = theta / delta
    rho = 1.0 / sigma
    iterate = start
    residual = (rhs_v[...] - own_part(start)) - ghost_part(0)
    direction = residual * (inverse * (1.0 / theta))
    for step in range(STEPS):
        send_ghosts(step + 1, direction)
        iterate = iterate + direction
        rest = residual - own_part(direction)
        if step + 1 < STEPS:
            rho_new = 1.0 / (2.0 * sigma - rho)
            gain = (2.0 * rho_new / delta) * inverse
            kept = (rho_new * rho) * direction + gain * rest
            ghosts = ghost_part(step + 1)
            direction = kept - gain * ghosts
            residual = rest - ghosts
            rho = rho_new
        else:
            out_ref[0] = iterate
            residual = rest - ghost_part(step + 1)

    squares = jnp.sum((residual * residual).T, axis=0, keepdims=True)
    part = jnp.concatenate([squares, jnp.zeros((1, 128 - width), jnp.float32)], axis=1)
    sent = []
    for buf, ss, rs, here, count, peer in (
        (red_g, red_g_ss, red_g_rs, grp, ng, g_peer),
        (red_x, red_x_ss, red_x_rs, x, nx, x_peer),
        (red_z, red_z_ss, red_z_rs, z, nz, z_peer),
    ):
        buf[here] = part
        copies = [
            pltpu.make_async_remote_copy(
                src_ref=buf.at[here], dst_ref=buf.at[here],
                send_sem=ss.at[k - 1], recv_sem=rs.at[k - 1],
                device_id=peer(k), device_id_type=MESH,
            )
            for k in range(1, count)
        ]
        for copy in copies:
            copy.start()
        for k in range(1, count):
            other = lax.rem(here + count - k, count)
            pltpu.make_async_remote_copy(
                src_ref=buf.at[here], dst_ref=buf.at[other],
                send_sem=ss.at[k - 1], recv_sem=rs.at[k - 1],
                device_id=peer(k), device_id_type=MESH,
            ).wait_recv()
        part = buf[0]
        for k in range(1, count):
            part = part + buf[k]
        sent += copies
    rms_ref[...] = jnp.sqrt(part * (1.0 / (ng * ndev * 128)))[:, :width]

    for copy in sent:
        copy.wait_send()
    for n in range(STEPS + 1):
        for copy in ghost_copies(n):
            copy.wait_send()
    for way in range(2):
        pl_copy(way).wait_send()
        for k in range(nk):
            leaf_copy(way, k).wait_send()
            for h in halves(way, k):
                for copy in chain_copies(way, k, h):
                    copy.wait_send()
    for j in range(1, nx):
        po_copy(j).wait_send()
        pq_copy(j).wait_send()
        for k in range(nk):
            relay_copy(j, k).wait_send()
            for fam in range(2):
                own_copy(j, k, fam).wait_send()


def shards(ng, nx, nz, tiles, owner, tile_rows, tile_cols, ghost_rows, rhs, start, diag):
    tcount, block = tiles.shape[1], tiles.shape[2]
    width = rhs.shape[1]
    nk = nz // 4
    f32, bf16, i32, i16 = jnp.float32, jnp.bfloat16, jnp.int32, jnp.int16
    vmem, smem, dma = pltpu.VMEM, pltpu.SMEM, pltpu.SemaphoreType.DMA
    whole = pl.BlockSpec(memory_space=pltpu.VMEM)
    smoothed, rms = pl.pallas_call(
        functools.partial(kernel, ng, nx, nz),
        out_shape=(
            jax.ShapeDtypeStruct((1, width, 128), f32),
            jax.ShapeDtypeStruct((1, width), f32),
        ),
        in_specs=[pl.BlockSpec(memory_space=pltpu.HBM)] * 8,
        out_specs=(whole, whole),
        scratch_shapes=[
            smem((1, tcount), i32),
            smem((1, tcount), i32),
            smem((1, tcount), i32),
            smem((1, 2), i32),
            vmem((tcount, block, block), bf16),
            vmem((width, 128), f32),
            vmem((width, 128), f32),
            vmem((1, 128), f32),
            vmem((8, 128), i32),
            smem((8, 128), i32),
            vmem((nx, 2 * nk, 128), i32),
            vmem((nx, 2 * nk, 128), i32),
            vmem((2, nx, nk, 128), i32),
            vmem((2, nx, nk, 128), i32),
            vmem((nx, 2, nk, 128), i32),
            vmem((nx, nk, 2, 64, 128), bf16),
            vmem((nx, nk, 2, 64, 128), bf16),
            vmem((2, nk, nx, 64, 128), bf16),
            vmem((nk, 2, nx, 64, 128), bf16),
            vmem((nx, nk, 2, 64, 128), bf16),
            vmem((2, CH, 64, 128), f32),
            vmem((2, nk, 2, 2, 64, 128), i16),
            vmem((2, nk, 2, 2, 64, 128), i16),
            vmem((2, nk, 2, 2, 128), f32),
            vmem((2, nk, 2, 2, 128), f32),
            vmem((256, 256), bf16),
            vmem((STEPS + 1, width, 128), bf16),
            vmem((STEPS + 1, 2, width, 128), bf16),
            vmem((ng, 1, 128), f32),
            vmem((nx, 1, 128), f32),
            vmem((nz, 1, 128), f32),
            dma((8,)),
            dma,
            dma((nx - 1,)),
            dma((nx - 1,)),
            dma((2,)),
            dma((2,)),
            dma((nx - 1,)),
            dma((nx - 1,)),
            dma((nx - 1, nk, 2)),
            dma((nx - 1, nk, 2)),
            dma((2, nk)),
            dma((2, nk)),
            dma((nx - 1, nk)),
            dma((nx - 1, nk)),
            dma((2, nk, 2)),
            dma((2, nk, 2)),
            dma((2, nk, 2)),
            dma((2, nk, 2)),
            dma((STEPS + 1, 2)),
            dma((STEPS + 1, 2)),
            dma((ng - 1,)),
            dma((ng - 1,)),
            dma((nx - 1,)),
            dma((nx - 1,)),
            dma((nz - 1,)),
            dma((nz - 1,)),
        ],
        compiler_params=pltpu.CompilerParams(
            collective_id=0, has_side_effects=True, vmem_limit_bytes=32 * 1024 * 1024
        ),
    )(owner.reshape(1, tcount), tile_rows, tile_cols, ghost_rows, tiles, rhs, start, diag)
    return smoothed, rms.reshape(width)


def solution(mesh):
    ng = mesh.shape["grp"]
    nx = mesh.shape["dev"] // NZ
    return jax.shard_map(
        functools.partial(shards, ng, nx, NZ),
        mesh=mesh,
        in_specs=(
            P("grp", "dev", None, None),
            P("grp", "dev", None),
            P("grp", "dev"),
            P("grp", "dev"),
            P("grp", "dev"),
            P("grp", None, "dev"),
            P("grp", None, "dev"),
            P("grp", "dev"),
        ),
        out_specs=(P("grp", None, "dev"), P()),
        check_vma=False,
    )
```

time: 84.1 us -> 72.5 us (0.86)
  Pallas kernels: 77.2 us -> 65.8 us
    pallas_call x1, Pallas kernels: 77.2 us -> 65.8 us  [shards(): pl.pallas_call(functools.partial(kernel, ng, nx, nz), out_shape=(jax.Shap...]
where the time goes in v2:
time: 72.5 us; the launch traced here: 72.2 us
  Pallas kernels  65.8 us (91%)
  local copies, waits for them, and re-layouts  5.69 us (8%)
    pallas_call x1, Pallas kernels, shards(): pl.pallas_call(functools.partial(kernel, ng, nx, nz), out_shape=(jax.Shap...  65.8 us
    unnamed x18, local copies, waits for them, and re-layouts  5.69 us

profile of v2, /device:TPU:1, one launch (start us, length us, event | category | flops | bytes accessed | tf_op | source)
XLA Modules:
  0.0 72.2 jit_solution(13915927992491797377)
XLA Ops:
  0.6 0.0 copy-start.5
  0.6 0.0 copy-start.4
  0.7 0.0 copy-start.3
  0.7 0.6 copy-done.5
  1.3 0.0 copy-done.4
  1.3 0.0 copy-done.3
  1.3 0.0 copy-start
  1.3 1.2 %copy-done = bf16[1,54,64,64]{3,2,1,0:T(8,128)(2,1)S(1)} copy-done((bf16[1,54,64,64]{3,2,1,0:T(8,128)(2,1)S(1)}, bf16[1,54,64,64]{3,2,1,0:T(8,128)(2,1)}, u32[]{:S(2)}) %copy-start) | copy-done | bytes 442392
  2.5 0.0 copy-start.1
  2.5 0.7 copy-done.1
  3.2 0.0 copy-start.2
  3.2 0.7 copy-done.2
  3.9 0.0 copy-start.6
  3.9 0.7 copy-done.6
  4.6 0.0 copy-start.7
  4.6 0.7 copy-done.7
  5.2 65.8 %shard_map.95 = (f32[1,32,128]{2,1,0:T(8,128)S(1)}, f32[1,32]{1,0:T(1,128)S(1)}) custom-call(s32[1,54]{1,0:T(1,128)S(1)} %bitcast.2, s32[1,54]{1,0:T(1,128)S(1)} %copy-done.4, s32[1,54]{1,0:T(1,128)S(1)} %copy-done.5, s32[1,2]{1,0:T(1,128)S(1)} %copy-done.6, bf16[1,54,64,64]{3,2,1,0:T(8,128)(2,1)S(1)} %copy-done, f32[1,32,128]{2,1,0:T(8,128)S(1)} %copy-done.1, ...), custom_call_target="tpu_custom_call" | custom-call | tf_op jit(solution)/shard_map/pallas_call | solution.py:425
  71.1 0.6 copy.12
  71.7 0.5 copy.13
Async XLA Ops:
  0.6 0.7 copy-start.5
  0.6 0.7 copy-start.4
  0.7 0.7 copy-start.3
  1.3 1.2 %copy-start = (bf16[1,54,64,64]{3,2,1,0:T(8,128)(2,1)S(1)}, bf16[1,54,64,64]{3,2,1,0:T(8,128)(2,1)}, u32[]{:S(2)}) copy-start(bf16[1,54,64,64]{3,2,1,0:T(8,128)(2,1)} %tiles_h.1) | copy-start | bytes 1327108
  2.5 0.7 copy-start.1
  3.2 0.7 copy-start.2
  3.9 0.7 copy-start.6
  4.6 0.7 copy-start.7

commit v3 on v2

--- a/solution.py
+++ b/solution.py
@@ -18,12 +18,12 @@
     owner_h, rows_h, cols_h, ghost_h, tiles_h, rhs_h, start_h, diag_h,
     out_ref, rms_ref,
     owner_s, rows_s, cols_s, ghost_s, tiles_v, rhs_v, start_v, diag_v,
-    tab_v, tab_s, po_send, po, pl_send, pl_recv, pq,
-    osend, xown, lsend, lrecv, xleaf, dmat, qsend, qrecv, ssend, srecv, wmat,
-    gsend, grecv, red_g, red_x, red_z,
-    in_sem, tab_sem, po_ss, po_rs, pl_ss, pl_rs, pq_ss, pq_rs,
-    o_ss, o_rs, l_ss, l_rs, y_ss, y_rs, q_ss, q_rs, s_ss, s_rs, g_ss, g_rs,
-    red_g_ss, red_g_rs, red_x_ss, red_x_rs, red_z_ss, red_z_rs,
+    tab_v, tab_s, po_send, po, pl_send, pl_recv, pf_send, pf_recv,
+    osend, xown, lsend, lrecv, fsend, frecv, dmat, qsend, qrecv, ssend, srecv, wmat,
+    gsend, grecv, red_p, red_z,
+    in_sem, tab_sem, po_ss, po_rs, pl_ss, pl_rs, pf_ss, pf_rs,
+    o_ss, o_rs, l_ss, l_rs, f_ss, f_rs, q_ss, q_rs, s_ss, s_rs, g_ss, g_rs,
+    red_p_ss, red_p_rs, red_z_ss, red_z_rs,
 ):
     half = nz // 2
     nk = half // 2
@@ -35,14 +35,17 @@
     x = lax.div(dev, nz)
     z = lax.rem(dev, nz)
 
-    def x_peer(j):
-        return {"dev": lax.rem(x + j, nx) * nz + z}
-
-    def z_peer(k):
-        return {"dev": x * nz + lax.rem(z + k + nz, nz)}
-
-    def g_peer(k):
-        return {"grp": lax.rem(grp + k, ng)}
+    def at(j, k):
+        return {"dev": lax.rem(x + j, nx) * nz + lax.rem(z + k + nz, nz)}
+
+    plane = grp * nx + x
+
+    def plane_peer(n):
+        there = lax.rem(plane + n, ng * nx)
+        return {"grp": lax.div(there, nx), "dev": lax.rem(there, nx) * nz + z}
+
+    def z_peer(n):
+        return at(0, n)
 
     upper = {"dev": lax.rem(dev + 1, ndev)}
     lower = {"dev": lax.rem(dev + ndev - 1, ndev)}
@@ -59,8 +62,10 @@
         fetch.start()
 
     barrier = pltpu.get_barrier_semaphore()
-    peers = [upper, lower, z_peer(1), z_peer(-1), z_peer(2), z_peer(-2)]
-    peers += [x_peer(j) for j in range(1, nx)] + [g_peer(k) for k in range(1, ng)]
+    peers = [upper, lower]
+    peers += [at(j, k) for j in range(nx) for k in (-1, 1)]
+    peers += [at(j, k) for j in range(nx) for k in (-2, 2)]
+    peers += [plane_peer(n) for n in range(1, ng * nx)]
     for peer in peers:
         pl.semaphore_signal(barrier, inc=1, device_id=peer, device_id_type=MESH)
 
@@ -117,9 +122,9 @@
         return lax.rem(x + j, nx) * nz + lax.rem(z + step + nz, nz)
 
     def own_step(fam, k):
-        if fam == 0:
-            return half - 2 * k
-        return 0 if k == 0 else 2 * k - half
+        if k == 0:
+            return 0
+        return half - 2 * k if fam == 0 else 2 * k - half
 
     def leaf_step(way, k):
         return half - 1 - 2 * k if way == 0 else 2 * k + 1 - half
@@ -131,89 +136,91 @@
         return jnp.where(lane < 64, tab_s[2, o], tab_s[3, o])
 
     def po_copy(j):
-        return remote(po_send.at[j], po.at[j], po_ss.at[j - 1], po_rs.at[j - 1], x_peer(j))
-
-    def pl_copy(way):
+        return remote(po_send.at[j], po.at[j], po_ss.at[j - 1], po_rs.at[j - 1], at(j, 0))
+
+    def pl_copy(way, j):
         return remote(
-            pl_send.at[way], pl_recv.at[way], pl_ss.at[way], pl_rs.at[way],
-            z_peer(1 if way == 0 else -1),
-        )
-
-    def pq_copy(j):
-        return remote(pl_recv.at[:, j], pq.at[j], pq_ss.at[j - 1], pq_rs.at[j - 1], x_peer(j))
-
-    def own_copy(j, k, fam):
+            pl_send.at[way, j], pl_recv.at[way, j], pl_ss.at[way, j], pl_rs.at[way, j],
+            at(j, 1 - 2 * way),
+        )
+
+    def pf_copy(j):
+        return remote(pf_send.at[j], pf_recv.at[j], pf_ss.at[j], pf_rs.at[j], at(j, 2 - 4 * (j % 2)))
+
+    def own_copy(j, k):
+        count = 1 if k == 0 else 2
         return remote(
-            osend.at[j, k, fam], xown.at[j, k, fam],
-            o_ss.at[j - 1, k, fam], o_rs.at[j - 1, k, fam], x_peer(j),
-        )
-
-    def leaf_copy(way, k):
+            osend.at[j, k, pl.ds(0, count)], xown.at[j, k, pl.ds(0, count)],
+            o_ss.at[j - 1, k], o_rs.at[j - 1, k], at(j, 0),
+        )
+
+    def leaf_copy(way, k, j):
         return remote(
-            lsend.at[way, k], lrecv.at[k, way], l_ss.at[way, k], l_rs.at[way, k],
-            z_peer(1 if way == 0 else -1),
-        )
-
-    def relay_copy(j, k):
-        return remote(
-            lrecv.at[k, :, j], xleaf.at[j, k], y_ss.at[j - 1, k], y_rs.at[j - 1, k], x_peer(j)
-        )
-
-    def pack_own(k, fam):
-        for j in list(range(1, nx)) + [0]:
-            both = pair(owner_of(j, own_step(fam, k)))
+            lsend.at[way, k, j], lrecv.at[way, k, j], l_ss.at[way, k, j], l_rs.at[way, k, j],
+            at(j, 1 - 2 * way),
+        )
+
+    def far_copy(j):
+        return remote(fsend.at[j], frecv.at[j], f_ss.at[j], f_rs.at[j], at(j, 2 - 4 * (j % 2)))
+
+    order = list(range(1, nx)) + [0]
+
+    def pack_own(k):
+        for j in order:
+            for fam in range(1 if k == 0 else 2):
+                both = pair(owner_of(j, own_step(fam, k)))
+                if j:
+                    osend[j, k, fam] = both
+                else:
+                    xown[0, k, fam] = both
             if j:
-                osend[j, k, fam] = both
-                own_copy(j, k, fam).start()
-            else:
-                xown[0, k, fam] = both
+                own_copy(j, k).start()
 
     def pack_leaf(k):
-        for way in range(2):
-            for j in range(nx):
+        for j in order:
+            for way in range(2):
                 lsend[way, k, j] = pair(owner_of(j, leaf_step(way, k)))
-            leaf_copy(way, k).start()
-
-    def relay(k):
-        for way in range(2):
-            leaf_copy(way, k).wait_recv()
-        if k == 0:
-            for way in range(2):
-                pl_copy(way).wait_recv()
-            for j in range(1, nx):
-                pq_copy(j).start()
-            pq[0] = pl_recv[:, 0]
-        for j in range(1, nx):
-            relay_copy(j, k).start()
-        xleaf[0, k] = lrecv[k, :, 0]
+                leaf_copy(way, k, j).start()
+
+    def pack_far():
+        for j in order:
+            fsend[j] = pair(owner_of(j, half))
+            far_copy(j).start()
 
     tab_copy.wait()
     fetches[4].wait()
     fetches[5].wait()
     start = start_v[...]
     for j in range(nx):
+        pf_send[j] = place(owner_of(j, half))
         for k in range(nk):
             for fam in range(2):
-                row = place(owner_of(j, own_step(fam, k)))
                 n = k * 2 + fam
-                if j:
-                    po_send[j, n:n + 1, :] = row
-                else:
-                    po[0, n:n + 1, :] = row
+                if n != 1:
+                    row = place(owner_of(j, own_step(fam, k)))
+                    if j:
+                        po_send[j, n:n + 1, :] = row
+                    else:
+                        po[0, n:n + 1, :] = row
                 pl_send[fam, j, k:k + 1, :] = place(owner_of(j, leaf_step(fam, k)))
+        if j:
+            po_send[j, 1:2, :] = none
+        else:
+            po[0, 1:2, :] = none
 
     pl.semaphore_wait(barrier, len(peers))
-    for j in range(1, nx):
-        po_copy(j).start()
-    pack_own(0, 0)
-    for way in range(2):
-        pl_copy(way).start()
-    pack_leaf(0)
+    for j in order:
+        pf_copy(j).start()
+        for way in range(2):
+            pl_copy(way, j).start()
+        if j:
+            po_copy(j).start()
+    pack_far()
     for k in range(1, nk):
-        pack_own(k, 0)
-        pack_own(k, 1)
-        pack_leaf(k)
-    pack_own(0, 1)
+        pack_leaf(k - 1)
+        pack_own(k)
+    pack_leaf(nk - 1)
+    pack_own(0)
     send_ghosts(0, start)
 
     right_half = (lane >= 64).astype(jnp.int32)
@@ -229,20 +236,26 @@
             out.append(value + jnp.where(row_swapped == target, swapped, 0.0))
         return tuple(out)
 
-    def dense(n, own, leaves):
-        k, fam = own
-        for j in range(1, nx):
-            own_copy(j, k, fam).wait_recv()
-
-        def column(j, acc):
-            acc = add_pair(acc, xown[j, k, fam], po[j, k * 2 + fam:k * 2 + fam + 1, :])
-            for way, kk in leaves:
-                acc = add_pair(acc, xleaf[j, kk, way], pq[j, way, kk:kk + 1, :])
-            return acc
-
-        acc = lax.fori_loop(
-            0, nx, column, tuple(jnp.zeros((64, 128), jnp.float32) for _ in range(CH))
-        )
+    def dense(n, k, fam, leaves, far):
+        acc = tuple(jnp.zeros((64, 128), jnp.float32) for _ in range(CH))
+        for j in far:
+            far_copy(j).wait_recv()
+            acc = add_pair(acc, frecv[j], pf_recv[j])
+
+        for way, kk in leaves:
+            def leaf(j, acc, way=way, kk=kk):
+                leaf_copy(way, kk, j).wait_recv()
+                return add_pair(acc, lrecv[way, kk, j], pl_recv[way, j, kk:kk + 1, :])
+
+            acc = lax.fori_loop(0, nx, leaf, acc)
+        if fam == 0:
+            for j in range(1, nx):
+                own_copy(j, k).wait_recv()
+
+        def own(j, acc):
+            return add_pair(acc, xown[j, k, fam], po[j, k * 2 + fam:k * 2 + fam + 1, :])
+
+        acc = lax.fori_loop(0, nx, own, acc)
         for c in range(CH):
             dmat[n, c] = acc[c]
 
@@ -272,41 +285,31 @@
         whole = qrecv[way, s, h, cp].astype(jnp.int32).astype(jnp.float32)
         return whole * srecv[way, s, h, cp:cp + 1, :]
 
-    def halves(way, s):
-        return (way,) if s == 0 else (0, 1)
-
     for j in range(1, nx):
         po_copy(j).wait_recv()
-    dense(0, (0, 0), ())
-    for way in range(2):
-        send_half(way, 0, way, [dmat[0, way * 2 + cp] for cp in range(2)])
-    for k in range(nk):
-        relay(k)
-        if k == 0:
-            for j in range(1, nx):
-                pq_copy(j).wait_recv()
-        for j in range(1, nx):
-            relay_copy(j, k).wait_recv()
-        s = k + 1
-        if s < nk:
+    for j in range(nx):
+        pf_copy(j).wait_recv()
+        for way in range(2):
+            pl_copy(way, j).wait_recv()
+    for s in range(1, nk):
+        for way in range(2):
+            far = [j for j in range(nx) if j % 2 == way] if s == 1 else []
+            dense(way, s, way, [(way, s - 1)], far)
+        for h in range(2):
             for way in range(2):
-                dense(way, (s, way), ((way, k),))
-            for h in range(2):
-                for way in range(2):
-                    values = [dmat[way, h * 2 + cp] for cp in range(2)]
-                    if h in halves(way, k):
-                        for copy in chain_copies(way, k, h):
-                            copy.wait_recv()
-                        values = [values[cp] + arrived(way, k, h, cp) for cp in range(2)]
-                    send_half(way, s, h, values)
-    dense(0, (0, 1), ((0, nk - 1), (1, nk - 1)))
+                values = [dmat[way, h * 2 + cp] for cp in range(2)]
+                if s > 1:
+                    for copy in chain_copies(way, s - 1, h):
+                        copy.wait_recv()
+                    values = [values[cp] + arrived(way, s - 1, h, cp) for cp in range(2)]
+                send_half(way, s, h, values)
+    dense(0, 0, 0, [(0, nk - 1), (1, nk - 1)], [])
     for h in range(2):
         values = [dmat[0, h * 2 + cp] for cp in range(2)]
         for way in range(2):
-            if h in halves(way, nk - 1):
-                for copy in chain_copies(way, nk - 1, h):
-                    copy.wait_recv()
-                values = [values[cp] + arrived(way, nk - 1, h, cp) for cp in range(2)]
+            for copy in chain_copies(way, nk - 1, h):
+                copy.wait_recv()
+            values = [values[cp] + arrived(way, nk - 1, h, cp) for cp in range(2)]
         for cp in range(2):
             high = values[cp].astype(jnp.bfloat16)
             low = (values[cp] - high.astype(jnp.float32)).astype(jnp.bfloat16)
@@ -366,8 +369,7 @@
     part = jnp.concatenate([squares, jnp.zeros((1, 128 - width), jnp.float32)], axis=1)
     sent = []
     for buf, ss, rs, here, count, peer in (
-        (red_g, red_g_ss, red_g_rs, grp, ng, g_peer),
-        (red_x, red_x_ss, red_x_rs, x, nx, x_peer),
+        (red_p, red_p_ss, red_p_rs, plane, ng * nx, plane_peer),
         (red_z, red_z_ss, red_z_rs, z, nz, z_peer),
     ):
         buf[here] = part
@@ -399,20 +401,23 @@
     for n in range(STEPS + 1):
         for copy in ghost_copies(n):
             copy.wait_send()
-    for way in range(2):
-        pl_copy(way).wait_send()
+    for j in range(nx):
+        far_copy(j).wait_send()
+        pf_copy(j).wait_send()
+        if j:
+            po_copy(j).wait_send()
+        for way in range(2):
+            pl_copy(way, j).wait_send()
         for k in range(nk):
-            leaf_copy(way, k).wait_send()
-            for h in halves(way, k):
-                for copy in chain_copies(way, k, h):
+            if j:
+                own_copy(j, k).wait_send()
+            for way in range(2):
+                leaf_copy(way, k, j).wait_send()
+    for s in range(1, nk):
+        for way in range(2):
+            for h in range(2):
+                for copy in chain_copies(way, s, h):
                     copy.wait_send()
-    for j in range(1, nx):
-        po_copy(j).wait_send()
-        pq_copy(j).wait_send()
-        for k in range(nk):
-            relay_copy(j, k).wait_send()
-            for fam in range(2):
-                own_copy(j, k, fam).wait_send()
 
 
 def shards(ng, nx, nz, tiles, owner, tile_rows, tile_cols, ghost_rows, rhs, start, diag):
@@ -445,12 +450,14 @@
             vmem((nx, 2 * nk, 128), i32),
             vmem((2, nx, nk, 128), i32),
             vmem((2, nx, nk, 128), i32),
-            vmem((nx, 2, nk, 128), i32),
+            vmem((nx, 1, 128), i32),
+            vmem((nx, 1, 128), i32),
             vmem((nx, nk, 2, 64, 128), bf16),
             vmem((nx, nk, 2, 64, 128), bf16),
             vmem((2, nk, nx, 64, 128), bf16),
-            vmem((nk, 2, nx, 64, 128), bf16),
-            vmem((nx, nk, 2, 64, 128), bf16),
+            vmem((2, nk, nx, 64, 128), bf16),
+            vmem((nx, 64, 128), bf16),
+            vmem((nx, 64, 128), bf16),
             vmem((2, CH, 64, 128), f32),
             vmem((2, nk, 2, 2, 64, 128), i16),
             vmem((2, nk, 2, 2, 64, 128), i16),
@@ -459,38 +466,35 @@
             vmem((256, 256), bf16),
             vmem((STEPS + 1, width, 128), bf16),
             vmem((STEPS + 1, 2, width, 128), bf16),
-            vmem((ng, 1, 128), f32),
-            vmem((nx, 1, 128), f32),
+            vmem((ng * nx, 1, 128), f32),
             vmem((nz, 1, 128), f32),
             dma((8,)),
             dma,
             dma((nx - 1,)),
             dma((nx - 1,)),
-            dma((2,)),
-            dma((2,)),
-            dma((nx - 1,)),
-            dma((nx - 1,)),
-            dma((nx - 1, nk, 2)),
-            dma((nx - 1, nk, 2)),
-            dma((2, nk)),
-            dma((2, nk)),
+            dma((2, nx)),
+            dma((2, nx)),
+            dma((nx,)),
+            dma((nx,)),
             dma((nx - 1, nk)),
             dma((nx - 1, nk)),
+            dma((2, nk, nx)),
+            dma((2, nk, nx)),
+            dma((nx,)),
+            dma((nx,)),
             dma((2, nk, 2)),
             dma((2, nk, 2)),
             dma((2, nk, 2)),
             dma((2, nk, 2)),
             dma((STEPS + 1, 2)),
             dma((STEPS + 1, 2)),
-            dma((ng - 1,)),
-            dma((ng - 1,)),
-            dma((nx - 1,)),
-            dma((nx - 1,)),
+            dma((ng * nx - 1,)),
+            dma((ng * nx - 1,)),
             dma((nz - 1,)),
             dma((nz - 1,)),
         ],
         compiler_params=pltpu.CompilerParams(
-            collective_id=0, has_side_effects=True, vmem_limit_bytes=32 * 1024 * 1024
+            collective_id=0, has_side_effects=True, vmem_limit_bytes=60 * 1024 * 1024
         ),
     )(owner.reshape(1, tcount), tile_rows, tile_cols, ghost_rows, tiles, rhs, start, diag)
     return smoothed, rms.reshape(width)

time: 72.5 us -> 70.7 us (0.975)
  local copies, waits for them, and re-layouts: 5.69 us -> 1.84 us
  Pallas kernels: 65.8 us -> 68.1 us
    unnamed x18 -> x4, local copies, waits for them, and re-layouts: 5.69 us -> 1.84 us
    pallas_call x1, Pallas kernels: 65.8 us -> 68.1 us  [shards(): pl.pallas_call(functools.partial(kernel, ng, nx, nz), out_shape=(jax.Shap...]
where the time goes in v3:
time: 70.7 us; the launch traced here: 70.6 us
  Pallas kernels  68.1 us (96%)
  local copies, waits for them, and re-layouts  1.84 us (3%)
    pallas_call x1, Pallas kernels, shards(): pl.pallas_call(functools.partial(kernel, ng, nx, nz), out_shape=(jax.Shap...  68.1 us
    unnamed x4, local copies, waits for them, and re-layouts  1.84 us

profile of v3, /device:TPU:1, one launch (start us, length us, event | category | flops | bytes accessed | tf_op | source)
XLA Modules:
  0.0 70.6 jit_solution(8873551742324191815)
XLA Ops:
  0.6 68.1 %shard_map.95 = (f32[1,32,128]{2,1,0:T(8,128)}, f32[1,32]{1,0:T(1,128)}) custom-call(s32[1,54]{1,0:T(1,128)} %bitcast.2, s32[1,54]{1,0:T(1,128)} %rows_h.1, s32[1,54]{1,0:T(1,128)} %cols_h.1, s32[1,2]{1,0:T(1,128)} %ghost_h.1, bf16[1,54,64,64]{3,2,1,0:T(8,128)(2,1)} %tiles_h.1, f32[1,32,128]{2,1,0:T(8,128)} %rhs_h.1, f32[1,32,128]{2,1,0:T(8,128)} %start_h.1, ...), custom_call_target="tpu_custom_call" | custom-call | tf_op jit(solution)/shard_map/pallas_call | solution.py:430
  68.7 0.0 copy-start
  68.7 1.3 %copy.12 = f32[1,32,128]{2,1,0:T(8,128)} copy(f32[1,32,128]{2,1,0:T(8,128)} %get-tuple-element.8) | data formatting | bytes 32768
  70.0 0.0 copy-done
  70.0 0.5 copy.13
Async XLA Ops:
  68.7 1.3 %copy-start = (f32[1,32]{1,0:T(1,128)S(1)}, f32[1,32]{1,0:T(1,128)}, u32[]{:S(2)}) copy-start(f32[1,32]{1,0:T(1,128)} %get-tuple-element.5) | copy-start | bytes 388

commit v4 on v3

v4 whole, which is shorter than its diff:
```python
import functools

import jax
import jax.numpy as jnp
from jax import lax
from jax.experimental import pallas as pl
from jax.experimental.pallas import tpu as pltpu
from jax.sharding import PartitionSpec as P

STEPS = 3
NZ = 16
CH = 4
MESH = pl.DeviceIdType.MESH


def kernel(
    ng, nx, nz,
    owner_h, rows_h, cols_h, ghost_h, tiles_h, rhs_h, start_h, diag_h,
    out_ref, rms_ref,
    owner_s, rows_s, cols_s, ghost_s, tiles_v, rhs_v, start_v, diag_v,
    tab_v, tab_s, psend, precv, bsend, xown, lrecv, frecv, dmat,
    qsend, qrecv, ssend, srecv, wmat, gsend, grecv, nsend, nrecv, wsend, wrecv, red_p, red_z,
    out_v, in_sem, tab_sem, out_sem, p_ss, p_rs, b_ss, o_rs, l_rs, f_rs,
    q_ss, q_rs, s_ss, s_rs, g_ss, g_rs, n_ss, n_rs, w_ss, w_rs,
    red_p_ss, red_p_rs, red_z_ss, red_z_rs,
):
    half = nz // 2
    nk = half // 2
    ndev = nx * nz
    tcount = tiles_v.shape[0]
    width = rhs_v.shape[0]
    dev = lax.axis_index("dev")
    grp = lax.axis_index("grp")
    x = lax.div(dev, nz)
    z = lax.rem(dev, nz)

    def at(j, k):
        return {"dev": lax.rem(x + j, nx) * nz + lax.rem(z + k + nz, nz)}

    plane = grp * nx + x

    def plane_peer(n):
        there = lax.rem(plane + n, ng * nx)
        return {"grp": lax.div(there, nx), "dev": lax.rem(there, nx) * nz + z}

    def z_peer(n):
        return at(0, n)

    upper = {"dev": lax.rem(dev + 1, ndev)}
    lower = {"dev": lax.rem(dev + ndev - 1, ndev)}
    upper2 = {"dev": lax.rem(dev + 2, ndev)}
    lower2 = {"dev": lax.rem(dev + ndev - 2, ndev)}

    fetches = [
        pltpu.make_async_copy(src, dst, in_sem.at[n])
        for n, (src, dst) in enumerate((
            (owner_h, owner_s), (rows_h, rows_s), (cols_h, cols_s), (ghost_h, ghost_s),
            (tiles_h.at[0], tiles_v), (start_h.at[0], start_v), (rhs_h.at[0], rhs_v),
            (diag_h, diag_v),
        ))
    ]
    for fetch in fetches:
        fetch.start()

    barrier = pltpu.get_barrier_semaphore()
    peers = [upper, lower, upper2, lower2]
    peers += [at(j, k) for j in range(nx) for k in (-1, 1)]
    peers += [at(j, k) for j in range(nx) for k in (-2, 2)]
    peers += [plane_peer(n) for n in range(1, ng * nx)]
    for peer in peers:
        pl.semaphore_signal(barrier, inc=1, device_id=peer, device_id_type=MESH)

    lane = lax.broadcasted_iota(jnp.int32, (1, 128), 1)
    none = jnp.full((1, 128), -1, jnp.int32)
    for fetch in fetches[:4]:
        fetch.wait()

    def find(t, held):
        i0, i1, p0, p1 = held
        hit = lane == owner_s[0, t]
        place = rows_s[0, t] * 4 + cols_s[0, t]
        first = jnp.logical_and(hit, i0 < 0)
        second = jnp.logical_and(hit, i0 >= 0)
        return (
            jnp.where(first, t, i0), jnp.where(second, t, i1),
            jnp.where(first, place, p0), jnp.where(second, place, p1),
        )

    i0, i1, p0, p1 = lax.fori_loop(0, tcount, find, (none,) * 4, unroll=True)
    tab_v[0:1, :] = jnp.maximum(i0, 0)
    tab_v[1:2, :] = jnp.maximum(i1, 0)
    tab_v[2:3, :] = p0
    tab_v[3:4, :] = p1
    tab_copy = pltpu.make_async_copy(tab_v, tab_s, tab_sem)
    tab_copy.start()

    wide = lax.broadcasted_iota(jnp.int32, (width, 128), 1)
    left = wide < 64
    stay = jnp.where(left, ghost_s[0, 1], 1 - ghost_s[0, 0]) == 0

    def pack_ghosts(vec):
        return jnp.where(stay[:vec.shape[0]], vec, pltpu.roll(vec, 64, 1))

    def remote(src, dst, ss, rs, peer):
        return pltpu.make_async_remote_copy(
            src_ref=src, dst_ref=dst, send_sem=ss, recv_sem=rs,
            device_id=peer, device_id_type=MESH,
        )

    def wait_bytes(ref, sem):
        pltpu.make_async_copy(ref, ref, sem).wait()

    def send_ghosts(n, vec):
        gsend[n] = pack_ghosts(vec).astype(jnp.bfloat16)
        for way, peer in enumerate((upper, lower)):
            remote(gsend.at[n], grecv.at[2 * n + way], g_ss, g_rs.at[n], peer).start()

    def owner_of(j, step):
        return lax.rem(x + j, nx) * nz + lax.rem(z + step + nz, nz)

    def own_step(fam, k):
        if k == 0:
            return 0
        return half - 2 * k if fam == 0 else 2 * k - half

    def leaf_step(way, k):
        return half - 1 - 2 * k if way == 0 else 2 * k + 1 - half

    def pair(o):
        return jnp.concatenate([tiles_v[tab_s[0, o]], tiles_v[tab_s[1, o]]], axis=1)

    def place(o):
        return jnp.where(lane < 64, tab_s[2, o], tab_s[3, o])

    oc = 2 * nk - 1
    leaf_row, far_row = nx * oc, nx * oc + 2 * nx * nk
    leaf_slot, own_slot = nx, nx + 2 * nk * nx

    def own_index(k, fam):
        return oc - 1 if k == 0 else 2 * (k - 1) + fam

    order = list(range(1, nx)) + [0]

    def send_places():
        for j in order:
            spans = [
                (leaf_row + (way * nx + j) * nk, nk, at(j, 1 - 2 * way)) for way in range(2)
            ]
            spans.append((far_row + j, 1, at(j, 2 - 4 * (j % 2))))
            if j:
                spans.append((j * oc, oc, at(j, 0)))
            for first, count, peer in spans:
                rows = pl.ds(first, count)
                remote(psend.at[rows], precv.at[rows], p_ss, p_rs, peer).start()

    def send_far():
        for j in order:
            remote(
                bsend.at[j], frecv.at[j], b_ss, f_rs.at[j % 2], at(j, 2 - 4 * (j % 2))
            ).start()

    def send_leaf(k):
        for j in order:
            for way in range(2):
                slot = leaf_slot + (way * nk + k) * nx + j
                remote(
                    bsend.at[slot], lrecv.at[way, k, j], b_ss, l_rs.at[way, k],
                    at(j, 1 - 2 * way),
                ).start()

    def send_own(k):
        count = 1 if k == 0 else 2
        for j in range(1, nx):
            slot = own_slot + (j - 1) * oc + own_index(k, 0)
            remote(
                bsend.at[pl.ds(slot, count)], xown.at[j, pl.ds(own_index(k, 0), count)],
                b_ss, o_rs.at[k], at(j, 0),
            ).start()

    tab_copy.wait()
    fetches[4].wait()
    fetches[5].wait()
    start = start_v[...]
    for j in range(nx):
        o = owner_of(j, half)
        psend[far_row + j] = place(o)
        bsend[j] = pair(o)
        for k in range(nk):
            for way in range(2):
                o = owner_of(j, leaf_step(way, k))
                psend[leaf_row + (way * nx + j) * nk + k] = place(o)
                bsend[leaf_slot + (way * nk + k) * nx + j] = pair(o)
            for fam in range(1 if k == 0 else 2):
                o = owner_of(j, own_step(fam, k))
                n = own_index(k, fam)
                if j:
                    psend[j * oc + n] = place(o)
                    bsend[own_slot + (j - 1) * oc + n] = pair(o)
                else:
                    precv[n] = place(o)
                    xown[0, n] = pair(o)

    pl.semaphore_wait(barrier, len(peers))
    send_far()
    send_leaf(0)
    send_own(1)
    send_places()
    for k in range(1, nk):
        send_leaf(k)
        send_own((k + 1) % nk)
    send_ghosts(0, start)

    right_half = (lane >= 64).astype(jnp.int32)

    def add_pair(acc, both, row):
        both = both.astype(jnp.float32)
        swapped = pltpu.roll(both, 64, 1)
        row_swapped = pltpu.roll(row, 64, 1)
        out = []
        for c in range(CH):
            target = (c // 2) * 4 + (c % 2) * 2 + right_half
            value = acc[c] + jnp.where(row == target, both, 0.0)
            out.append(value + jnp.where(row_swapped == target, swapped, 0.0))
        return tuple(out)

    def dense(n, k, fam, leaves, far):
        acc = tuple(jnp.zeros((64, 128), jnp.float32) for _ in range(CH))
        if far:
            wait_bytes(frecv.at[pl.ds(0, len(far))], f_rs.at[fam])
        for j in far:
            acc = add_pair(acc, frecv[j], precv[far_row + j])
        for way, kk in leaves:
            wait_bytes(lrecv.at[way, kk], l_rs.at[way, kk])
            for j in range(nx):
                row = leaf_row + (way * nx + j) * nk + kk
                acc = add_pair(acc, lrecv[way, kk, j], precv[row])
        if fam == 0:
            count = 1 if k == 0 else 2
            wait_bytes(
                xown.at[pl.ds(1, nx - 1), pl.ds(own_index(k, 0), count)], o_rs.at[k]
            )
        for j in range(nx):
            i = own_index(k, fam)
            acc = add_pair(acc, xown[j, i], precv[j * oc + i])
        for c in range(CH):
            dmat[n, c] = acc[c]

    def chain_copies(way, s, h):
        peer = z_peer(2 if way == 0 else -2)
        n = s - 1
        return (
            remote(ssend.at[way, n, h], srecv.at[way, n, h], s_ss, s_rs.at[way, n, h], peer),
            remote(qsend.at[way, n, h], qrecv.at[way, n, h], q_ss, q_rs.at[way, n, h], peer),
        )

    def send_half(way, s, h, values):
        for cp in range(2):
            most = jnp.maximum(jnp.max(jnp.abs(values[cp]), axis=0, keepdims=True), 1e-30)
            scaled = jnp.round(values[cp] * (32767.0 / most))
            qsend[way, s - 1, h, cp] = scaled.astype(jnp.int32).astype(jnp.int16)
            ssend[way, s - 1, h, cp:cp + 1, :] = most * (1.0 / 32767.0)
        for copy in chain_copies(way, s, h):
            copy.start()

    def arrived(way, s, h, cp):
        whole = qrecv[way, s - 1, h, cp].astype(jnp.int32).astype(jnp.float32)
        return whole * srecv[way, s - 1, h, cp:cp + 1, :]

    wait_bytes(precv.at[pl.ds(oc, far_row + nx - oc)], p_rs)
    for s in range(1, nk):
        for way in range(2):
            far = [j for j in range(nx) if j % 2 == way] if s == 1 else []
            dense(way, s, way, [(way, s - 1)], far)
        for h in range(2):
            for way in range(2):
                values = [dmat[way, h * 2 + cp] for cp in range(2)]
                if s > 1:
                    for copy in chain_copies(way, s - 1, h):
                        copy.wait_recv()
                    values = [values[cp] + arrived(way, s - 1, h, cp) for cp in range(2)]
                send_half(way, s, h, values)
    dense(0, 0, 0, [(0, nk - 1), (1, nk - 1)], [])
    ghost_rows = []
    for h in range(2):
        values = [dmat[0, h * 2 + cp] for cp in range(2)]
        for way in range(2):
            for copy in chain_copies(way, nk - 1, h):
                copy.wait_recv()
            values = [values[cp] + arrived(way, nk - 1, h, cp) for cp in range(2)]
        for cp in range(2):
            high = values[cp].astype(jnp.bfloat16)
            low = (values[cp] - high.astype(jnp.float32)).astype(jnp.bfloat16)
            wmat[h * 64:h * 64 + 64, cp * 128:cp * 128 + 128] = high
            wmat[128 + h * 64:192 + h * 64, cp * 128:cp * 128 + 128] = low
        ghost_rows.append(values[1])

    for way, peer in enumerate((upper, lower)):
        chosen = jnp.where(ghost_s[0, 1 - way] == 0, ghost_rows[0], ghost_rows[1])
        high = chosen.astype(jnp.bfloat16)
        nsend[way, 0:64, :] = high
        nsend[way, 64:128, :] = (chosen - high.astype(jnp.float32)).astype(jnp.bfloat16)
        remote(nsend.at[way], nrecv.at[way], n_ss, n_rs, peer).start()

    fetches[6].wait()
    fetches[7].wait()
    diag = diag_v[...]
    inverse = 1.0 / diag
    from_lower = jnp.logical_and(left, dev > 0)
    from_upper = jnp.logical_and(jnp.logical_not(left), dev < ndev - 1)

    def product(vec, columns):
        both = lax.dot_general(
            vec.astype(jnp.bfloat16), wmat[:, columns:columns + 128],
            (((1,), (1,)), ((), ())), preferred_element_type=jnp.float32,
        )
        return both[:, :128] + both[:, 128:]

    def own_part(vec):
        return diag * vec + product(vec, 0)

    def ghost_part(n):
        wait_bytes(grecv.at[pl.ds(2 * n, 2)], g_rs.at[n])
        ghosts = jnp.where(from_lower, grecv[2 * n].astype(jnp.float32), 0.0)
        ghosts = jnp.where(from_upper, grecv[2 * n + 1].astype(jnp.float32), ghosts)
        return product(ghosts, 128)

    def neighbour_part(vec, way):
        both = lax.dot_general(
            vec.astype(jnp.bfloat16), nrecv[way], (((1,), (1,)), ((), ())),
            preferred_element_type=jnp.float32,
        )
        return both + pltpu.roll(both, 64, 1)

    def next_ghosts(mine):
        far = jnp.where(
            jnp.logical_and(left, dev > 1), grecv[6].astype(jnp.float32), 0.0
        )
        below = jnp.where(left, far, mine)
        far = jnp.where(
            jnp.logical_and(jnp.logical_not(left), dev < ndev - 2),
            grecv[7].astype(jnp.float32), 0.0,
        )
        above = jnp.where(left, mine, far)
        summed = jnp.where(left, neighbour_part(below, 0), neighbour_part(above, 1))
        kept = jnp.where(left, wrecv[0, 0:width, :], wrecv[1, 0:width, :])
        scale = jnp.where(
            left[:8], wrecv[0, width:width + 8, :], wrecv[1, width:width + 8, :]
        )[0:1]
        ghosts = kept - scale * summed
        return jnp.where(jnp.logical_or(from_lower, from_upper), ghosts, 0.0)

    lmax = 2.0
    lmin = 0.2
    theta = (lmax + lmin) / 2.0
    delta = (lmax - lmin) / 2.0
    sigma = theta / delta
    rho = 1.0 / sigma
    iterate = start
    residual = (rhs_v[...] - own_part(start)) - ghost_part(0)
    direction = residual * (inverse * (1.0 / theta))
    for step in range(1, STEPS):
        send_ghosts(step, direction)
        if step == STEPS - 1:
            remote(gsend.at[step], grecv.at[6], g_ss, g_rs.at[STEPS], upper2).start()
            remote(gsend.at[step], grecv.at[7], g_ss, g_rs.at[STEPS], lower2).start()
        iterate = iterate + direction
        rest = residual - own_part(direction)
        rho_new = 1.0 / (2.0 * sigma - rho)
        gain = (2.0 * rho_new / delta) * inverse
        kept = (rho_new * rho) * direction + gain * rest
        if step == STEPS - 1:
            wsend[0:width, :] = pack_ghosts(kept)
            wsend[width:width + 8, :] = pack_ghosts(jnp.broadcast_to(gain, (8, 128)))
            for way, peer in enumerate((upper, lower)):
                remote(wsend, wrecv.at[way], w_ss, w_rs, peer).start()
        ghosts = ghost_part(step)
        direction = kept - gain * ghosts
        residual = rest - ghosts
        rho = rho_new
    out_v[...] = iterate + direction
    out_copy = pltpu.make_async_copy(out_v, out_ref.at[0], out_sem)
    out_copy.start()
    rest = residual - own_part(direction)
    wait_bytes(nrecv, n_rs)
    wait_bytes(grecv.at[pl.ds(6, 2)], g_rs.at[STEPS])
    wait_bytes(wrecv, w_rs)
    residual = rest - product(next_ghosts(gsend[STEPS - 1].astype(jnp.float32)), 128)

    squares = jnp.sum((residual * residual).T, axis=0, keepdims=True)
    part = jnp.concatenate([squares, jnp.zeros((1, 128 - width), jnp.float32)], axis=1)
    for buf, ss, rs, here, count, peer in (
        (red_p, red_p_ss, red_p_rs, plane, ng * nx, plane_peer),
        (red_z, red_z_ss, red_z_rs, z, nz, z_peer),
    ):
        buf[here] = part
        for n in range(1, count):
            remote(buf.at[here], buf.at[here], ss, rs, peer(n)).start()
        wait_bytes(buf.at[pl.ds(0, count - 1)], rs)
        part = buf[0]
        for n in range(1, count):
            part = part + buf[n]
    rms_ref[...] = jnp.sqrt(part * (1.0 / (ng * ndev * 128)))[:, :width]

    out_copy.wait()
    wait_bytes(psend.at[pl.ds(oc, far_row + nx - oc)], p_ss)
    wait_bytes(bsend, b_ss)
    wait_bytes(qsend, q_ss)
    wait_bytes(ssend, s_ss)
    wait_bytes(grecv, g_ss)
    wait_bytes(nsend, n_ss)
    wait_bytes(wrecv, w_ss)
    wait_bytes(red_p.at[pl.ds(0, ng * nx - 1)], red_p_ss)
    wait_bytes(red_z.at[pl.ds(0, nz - 1)], red_z_ss)


def shards(ng, nx, nz, tiles, owner, tile_rows, tile_cols, ghost_rows, rhs, start, diag):
    tcount, block = tiles.shape[1], tiles.shape[2]
    width = rhs.shape[1]
    nk = nz // 4
    f32, bf16, i32, i16 = jnp.float32, jnp.bfloat16, jnp.int32, jnp.int16
    vmem, smem, dma = pltpu.VMEM, pltpu.SMEM, pltpu.SemaphoreType.DMA
    whole = pl.BlockSpec(memory_space=pltpu.VMEM)
    smoothed, rms = pl.pallas_call(
        functools.partial(kernel, ng, nx, nz),
        out_shape=(
            jax.ShapeDtypeStruct((1, width, 128), f32),
            jax.ShapeDtypeStruct((1, width), f32),
        ),
        in_specs=[pl.BlockSpec(memory_space=pltpu.HBM)] * 8,
        out_specs=(pl.BlockSpec(memory_space=pltpu.HBM), whole),
        scratch_shapes=[
            smem((1, tcount), i32),
            smem((1, tcount), i32),
            smem((1, tcount), i32),
            smem((1, 2), i32),
            vmem((tcount, block, block), bf16),
            vmem((width, 128), f32),
            vmem((width, 128), f32),
            vmem((1, 128), f32),
            vmem((8, 128), i32),
            smem((8, 128), i32),
            vmem((nx * (4 * nk), 1, 128), i32),
            vmem((nx * (4 * nk), 1, 128), i32),
            vmem((nx + 2 * nk * nx + (nx - 1) * (2 * nk - 1), 64, 128), bf16),
            vmem((nx, 2 * nk - 1, 64, 128), bf16),
            vmem((2, nk, nx, 64, 128), bf16),
            vmem((nx, 64, 128), bf16),
            vmem((2, CH, 64, 128), f32),
            vmem((2, nk - 1, 2, 2, 64, 128), i16),
            vmem((2, nk - 1, 2, 2, 64, 128), i16),
            vmem((2, nk - 1, 2, 2, 128), f32),
            vmem((2, nk - 1, 2, 2, 128), f32),
            vmem((256, 256), bf16),
            vmem((STEPS, width, 128), bf16),
            vmem((2 * STEPS + 2, width, 128), bf16),
            vmem((2, 128, 128), bf16),
            vmem((2, 128, 128), bf16),
            vmem((width + 8, 128), f32),
            vmem((2, width + 8, 128), f32),
            vmem((ng * nx, 1, 128), f32),
            vmem((nz, 1, 128), f32),
            vmem((width, 128), f32),
            dma((8,)),
            dma,
            dma,
            dma,
            dma,
            dma,
            dma((nk,)),
            dma((2, nk)),
            dma((2,)),
            dma,
            dma((2, nk - 1, 2)),
            dma,
            dma((2, nk - 1, 2)),
            dma,
            dma((STEPS + 1,)),
            dma,
            dma,
            dma,
            dma,
            dma,
            dma,
            dma,
            dma,
        ],
        compiler_params=pltpu.CompilerParams(
            collective_id=0, has_side_effects=True, vmem_limit_bytes=60 * 1024 * 1024
        ),
    )(owner.reshape(1, tcount), tile_rows, tile_cols, ghost_rows, tiles, rhs, start, diag)
    return smoothed, rms.reshape(width)


def solution(mesh):
    ng = mesh.shape["grp"]
    nx = mesh.shape["dev"] // NZ
    return jax.shard_map(
        functools.partial(shards, ng, nx, NZ),
        mesh=mesh,
        in_specs=(
            P("grp", "dev", None, None),
            P("grp", "dev", None),
            P("grp", "dev"),
            P("grp", "dev"),
            P("grp", "dev"),
            P("grp", None, "dev"),
            P("grp", None, "dev"),
            P("grp", "dev"),
        ),
        out_specs=(P("grp", None, "dev"), P()),
        check_vma=False,
    )
```

time: 70.7 us -> 65.5 us (0.926)
  Pallas kernels: 68.1 us -> 62.9 us
    pallas_call x1, Pallas kernels: 68.1 us -> 62.9 us  [shards(): pl.pallas_call(functools.partial(kernel, ng, nx, nz), out_shape=(jax.Shap...]
where the time goes in v4:
time: 65.5 us; the launch traced here: 65.4 us
  Pallas kernels  62.9 us (96%)
  local copies, waits for them, and re-layouts  1.84 us (3%)
    pallas_call x1, Pallas kernels, shards(): pl.pallas_call(functools.partial(kernel, ng, nx, nz), out_shape=(jax.Shap...  62.9 us
    unnamed x4, local copies, waits for them, and re-layouts  1.84 us

profile of v4, /device:TPU:1, one launch (start us, length us, event | category | flops | bytes accessed | tf_op | source)
XLA Modules:
  0.0 65.4 jit_solution(12459823787779022989)
XLA Ops:
  0.6 62.9 %shard_map.95 = (f32[1,32,128]{2,1,0:T(8,128)}, f32[1,32]{1,0:T(1,128)}) custom-call(s32[1,54]{1,0:T(1,128)} %bitcast.2, s32[1,54]{1,0:T(1,128)} %rows_h.1, s32[1,54]{1,0:T(1,128)} %cols_h.1, s32[1,2]{1,0:T(1,128)} %ghost_h.1, bf16[1,54,64,64]{3,2,1,0:T(8,128)(2,1)} %tiles_h.1, f32[1,32,128]{2,1,0:T(8,128)} %rhs_h.1, f32[1,32,128]{2,1,0:T(8,128)} %start_h.1, ...), custom_call_target="tpu_custom_call" | custom-call | tf_op jit(solution)/shard_map/pallas_call | solution.py:423
  63.5 0.0 copy-start
  63.5 1.3 %copy.12 = f32[1,32,128]{2,1,0:T(8,128)} copy(f32[1,32,128]{2,1,0:T(8,128)} %get-tuple-element.8) | data formatting | bytes 32768
  64.9 0.0 copy-done
  64.9 0.5 copy.13
Async XLA Ops:
  63.5 1.3 %copy-start = (f32[1,32]{1,0:T(1,128)S(1)}, f32[1,32]{1,0:T(1,128)}, u32[]{:S(2)}) copy-start(f32[1,32]{1,0:T(1,128)} %get-tuple-element.5) | copy-start | bytes 388

commit v5 on v4

--- a/solution.py
+++ b/solution.py
@@ -205,9 +205,8 @@
     send_leaf(0)
     send_own(1)
     send_places()
-    for k in range(1, nk):
-        send_leaf(k)
-        send_own((k + 1) % nk)
+    send_leaf(1)
+    send_own(2 % nk)
     send_ghosts(0, start)
 
     right_half = (lane >= 64).astype(jnp.int32)
@@ -279,6 +278,9 @@
                         copy.wait_recv()
                     values = [values[cp] + arrived(way, s - 1, h, cp) for cp in range(2)]
                 send_half(way, s, h, values)
+        if s + 1 < nk:
+            send_leaf(s + 1)
+            send_own((s + 2) % nk)
     dense(0, 0, 0, [(0, nk - 1), (1, nk - 1)], [])
     ghost_rows = []
     for h in range(2):

time: 65.5 us -> 62.2 us (0.950)
  Pallas kernels: 62.9 us -> 59.5 us
    pallas_call x1, Pallas kernels: 62.9 us -> 59.5 us  [shards(): pl.pallas_call(functools.partial(kernel, ng, nx, nz), out_shape=(jax.Shap...]
where the time goes in v5:
time: 62.2 us; the launch traced here: 62 us
  Pallas kernels  59.5 us (96%)
  local copies, waits for them, and re-layouts  1.84 us (3%)
  between operations  0.65 us (1%)
    pallas_call x1, Pallas kernels, shards(): pl.pallas_call(functools.partial(kernel, ng, nx, nz), out_shape=(jax.Shap...  59.5 us
    unnamed x4, local copies, waits for them, and re-layouts  1.84 us

profile of v5, /device:TPU:1, one launch (start us, length us, event | category | flops | bytes accessed | tf_op | source)
XLA Modules:
  0.0 62.0 jit_solution(17315701531890657398)
XLA Ops:
  0.6 59.5 %shard_map.95 = (f32[1,32,128]{2,1,0:T(8,128)}, f32[1,32]{1,0:T(1,128)}) custom-call(s32[1,54]{1,0:T(1,128)} %bitcast.2, s32[1,54]{1,0:T(1,128)} %rows_h.1, s32[1,54]{1,0:T(1,128)} %cols_h.1, s32[1,2]{1,0:T(1,128)} %ghost_h.1, bf16[1,54,64,64]{3,2,1,0:T(8,128)(2,1)} %tiles_h.1, f32[1,32,128]{2,1,0:T(8,128)} %rhs_h.1, f32[1,32,128]{2,1,0:T(8,128)} %start_h.1, ...), custom_call_target="tpu_custom_call" | custom-call | tf_op jit(solution)/shard_map/pallas_call | solution.py:425
  60.2 0.0 copy-start
  60.2 1.3 %copy.12 = f32[1,32,128]{2,1,0:T(8,128)} copy(f32[1,32,128]{2,1,0:T(8,128)} %get-tuple-element.8) | data formatting | bytes 32768
  61.5 0.0 copy-done
  61.5 0.5 copy.13
Async XLA Ops:
  60.2 1.3 %copy-start = (f32[1,32]{1,0:T(1,128)S(1)}, f32[1,32]{1,0:T(1,128)}, u32[]{:S(2)}) copy-start(f32[1,32]{1,0:T(1,128)} %get-tuple-element.5) | copy-start | bytes 388

commit v6 on v5

--- a/solution.py
+++ b/solution.py
@@ -8,6 +8,9 @@
 from jax.sharding import PartitionSpec as P
 
 STEPS = 3
+THETA = (2.0 + 0.2) / 2.0
+DELTA = (2.0 - 0.2) / 2.0
+SIGMA = THETA / DELTA
 NZ = 16
 CH = 4
 MESH = pl.DeviceIdType.MESH
@@ -19,10 +22,10 @@
     out_ref, rms_ref,
     owner_s, rows_s, cols_s, ghost_s, tiles_v, rhs_v, start_v, diag_v,
     tab_v, tab_s, psend, precv, bsend, xown, lrecv, frecv, dmat,
-    qsend, qrecv, ssend, srecv, wmat, gsend, grecv, nsend, nrecv, wsend, wrecv, red_p, red_z,
-    out_v, in_sem, tab_sem, out_sem, p_ss, p_rs, b_ss, o_rs, l_rs, f_rs,
+    qsend, qrecv, ssend, srecv, wmat, gsend, grecv, nsend, nrecv, wsend, wrecv,
+    esend, erecv, pmat, ysend, yrecv, vsend, vrecv, red_c, red_p, red_z, out_v, in_sem, tab_sem, out_sem, p_ss, p_rs, b_ss, o_rs, l_rs, f_rs,
     q_ss, q_rs, s_ss, s_rs, g_ss, g_rs, n_ss, n_rs, w_ss, w_rs,
-    red_p_ss, red_p_rs, red_z_ss, red_z_rs,
+    e_ss, e_rs, y_ss, y_rs, v_ss, v_rs, red_c_ss, red_c_rs, red_p_ss, red_p_rs, red_z_ss, red_z_rs,
 ):
     half = nz // 2
     nk = half // 2
@@ -37,11 +40,17 @@
     def at(j, k):
         return {"dev": lax.rem(x + j, nx) * nz + lax.rem(z + k + nz, nz)}
 
-    plane = grp * nx + x
+    cores = 2 if ng % 2 == 0 else 1
+    core = lax.rem(grp, cores)
+    chips = ng // cores * nx
+    plane = lax.div(grp, cores) * nx + x
+
+    def core_peer(n):
+        return {"grp": grp + 1 - 2 * core}
 
     def plane_peer(n):
-        there = lax.rem(plane + n, ng * nx)
-        return {"grp": lax.div(there, nx), "dev": lax.rem(there, nx) * nz + z}
+        there = lax.rem(plane + n, chips)
+        return {"grp": lax.div(there, nx) * cores + core, "dev": lax.rem(there, nx) * nz + z}
 
     def z_peer(n):
         return at(0, n)
@@ -63,10 +72,11 @@
         fetch.start()
 
     barrier = pltpu.get_barrier_semaphore()
-    peers = [upper, lower, upper2, lower2]
-    peers += [at(j, k) for j in range(nx) for k in (-1, 1)]
-    peers += [at(j, k) for j in range(nx) for k in (-2, 2)]
-    peers += [plane_peer(n) for n in range(1, ng * nx)]
+    peers = [at(j, k) for j in range(nx) for k in (-1, 1)]
+    peers += [at(j, 0) for j in range(1, nx)] + [at(0, -2), at(0, 2)]
+    peers += [at(nx - j, 4 * (j % 2) - 2) for j in range(1, nx)]
+    peers += [upper, lower, upper2, lower2] + [core_peer(n) for n in range(1, cores)]
+    peers += [plane_peer(n) for n in range(1, chips)]
     for peer in peers:
         pl.semaphore_signal(barrier, inc=1, device_id=peer, device_id_type=MESH)
 
@@ -266,6 +276,26 @@
         return whole * srecv[way, s - 1, h, cp:cp + 1, :]
 
     wait_bytes(precv.at[pl.ds(oc, far_row + nx - oc)], p_rs)
+    def split(matrix, h, cp, value):
+        high = value.astype(jnp.bfloat16)
+        low = (value - high.astype(jnp.float32)).astype(jnp.bfloat16)
+        matrix[h * 64:h * 64 + 64, cp * 128:cp * 128 + 128] = high
+        matrix[128 + h * 64:192 + h * 64, cp * 128:cp * 128 + 128] = low
+
+    def times(vec, matrix):
+        both = lax.dot_general(
+            vec, matrix, (((1,), (1,)), ((), ())), preferred_element_type=jnp.float32
+        )
+        return both[:, :128] + both[:, 128:]
+
+    from_lower = jnp.logical_and(left, dev > 0)
+    from_upper = jnp.logical_and(jnp.logical_not(left), dev < ndev - 1)
+
+    def ghosts_of(n):
+        wait_bytes(grecv.at[pl.ds(2 * n, 2)], g_rs.at[n])
+        ghosts = jnp.where(from_lower, grecv[2 * n].astype(jnp.float32), 0.0)
+        return jnp.where(from_upper, grecv[2 * n + 1].astype(jnp.float32), ghosts)
+
     for s in range(1, nk):
         for way in range(2):
             far = [j for j in range(nx) if j % 2 == way] if s == 1 else []
@@ -278,10 +308,46 @@
                         copy.wait_recv()
                     values = [values[cp] + arrived(way, s - 1, h, cp) for cp in range(2)]
                 send_half(way, s, h, values)
+                if s == nk - 1:
+                    for cp in range(2):
+                        split(pmat.at[way], h, cp, values[cp])
+        if s == 1:
+            ghosts = ghosts_of(0)
+            esend[0:width, 0:128] = start.astype(jnp.bfloat16)
+            esend[0:width, 128:256] = ghosts.astype(jnp.bfloat16)
+            turned = jnp.broadcast_to(stay[0:1].astype(jnp.float32), (16, 128))
+            esend[width:width + 16, 0:128] = turned.astype(jnp.bfloat16)
+            esend[width:width + 16, 128:256] = turned.astype(jnp.bfloat16)
+            for way in range(2):
+                remote(esend, erecv.at[way], e_ss, e_rs, z_peer(2 * (2 * way - 1))).start()
         if s + 1 < nk:
             send_leaf(s + 1)
             send_own((s + 2) % nk)
+    wait_bytes(erecv, e_rs)
+    for way in range(2):
+        part = times(erecv[way, 0:width, :], pmat[way])
+        turned = erecv[way, width:width + 16, 0:128].astype(jnp.float32)[0:1]
+        ysend[way] = jnp.where(turned > 0.5, part, pltpu.roll(part, 64, 1))
+        first = lax.rem(z + 2 - 4 * way + nz, nz) + x * nz
+        for side in range(2):
+            remote(
+                ysend.at[way], yrecv.at[side, way], y_ss, y_rs,
+                {"dev": lax.rem(first + 1 - 2 * side + ndev, ndev)},
+            ).start()
+
     dense(0, 0, 0, [(0, nk - 1), (1, nk - 1)], [])
+    fetches[6].wait()
+    fetches[7].wait()
+    diag = diag_v[...]
+    inverse = 1.0 / diag
+    for c in range(CH):
+        split(wmat, c // 2, c % 2, dmat[0, c])
+    base = rhs_v[...] - diag * start
+    vsend[0:width, :] = pack_ghosts(base - times(esend[0:width, :], wmat[...]))
+    vsend[width:width + 8, :] = pack_ghosts(jnp.broadcast_to(inverse * (1.0 / THETA), (8, 128)))
+    for way, peer in enumerate((upper, lower)):
+        remote(vsend, vrecv.at[way], v_ss, v_rs, peer).start()
+
     ghost_rows = []
     for h in range(2):
         values = [dmat[0, h * 2 + cp] for cp in range(2)]
@@ -290,10 +356,7 @@
                 copy.wait_recv()
             values = [values[cp] + arrived(way, nk - 1, h, cp) for cp in range(2)]
         for cp in range(2):
-            high = values[cp].astype(jnp.bfloat16)
-            low = (values[cp] - high.astype(jnp.float32)).astype(jnp.bfloat16)
-            wmat[h * 64:h * 64 + 64, cp * 128:cp * 128 + 128] = high
-            wmat[128 + h * 64:192 + h * 64, cp * 128:cp * 128 + 128] = low
+            split(wmat, h, cp, values[cp])
         ghost_rows.append(values[1])
 
     for way, peer in enumerate((upper, lower)):
@@ -303,28 +366,26 @@
         nsend[way, 64:128, :] = (chosen - high.astype(jnp.float32)).astype(jnp.bfloat16)
         remote(nsend.at[way], nrecv.at[way], n_ss, n_rs, peer).start()
 
-    fetches[6].wait()
-    fetches[7].wait()
-    diag = diag_v[...]
-    inverse = 1.0 / diag
-    from_lower = jnp.logical_and(left, dev > 0)
-    from_upper = jnp.logical_and(jnp.logical_not(left), dev < ndev - 1)
-
     def product(vec, columns):
-        both = lax.dot_general(
-            vec.astype(jnp.bfloat16), wmat[:, columns:columns + 128],
-            (((1,), (1,)), ((), ())), preferred_element_type=jnp.float32,
-        )
-        return both[:, :128] + both[:, 128:]
+        return times(vec.astype(jnp.bfloat16), wmat[:, columns:columns + 128])
 
     def own_part(vec):
         return diag * vec + product(vec, 0)
 
-    def ghost_part(n):
-        wait_bytes(grecv.at[pl.ds(2 * n, 2)], g_rs.at[n])
-        ghosts = jnp.where(from_lower, grecv[2 * n].astype(jnp.float32), 0.0)
-        ghosts = jnp.where(from_upper, grecv[2 * n + 1].astype(jnp.float32), ghosts)
-        return product(ghosts, 128)
+    def mixed(ref):
+        return jnp.where(left, ref[0, 0:width, :], ref[1, 0:width, :])
+
+    def mixed_scale(ref):
+        return jnp.where(left[:8], ref[0, width:width + 8, :], ref[1, width:width + 8, :])[0:1]
+
+    def inside(ghosts):
+        return jnp.where(jnp.logical_or(from_lower, from_upper), ghosts, 0.0)
+
+    def first_ghosts():
+        wait_bytes(vrecv, v_rs)
+        wait_bytes(yrecv, y_rs)
+        parts = jnp.where(left, yrecv[0, 0] + yrecv[0, 1], yrecv[1, 0] + yrecv[1, 1])
+        return inside(mixed_scale(vrecv) * (mixed(vrecv) - parts))
 
     def neighbour_part(vec, way):
         both = lax.dot_general(
@@ -334,48 +395,37 @@
         return both + pltpu.roll(both, 64, 1)
 
     def next_ghosts(mine):
-        far = jnp.where(
-            jnp.logical_and(left, dev > 1), grecv[6].astype(jnp.float32), 0.0
-        )
+        far = jnp.where(jnp.logical_and(left, dev > 1), grecv[4].astype(jnp.float32), 0.0)
         below = jnp.where(left, far, mine)
         far = jnp.where(
             jnp.logical_and(jnp.logical_not(left), dev < ndev - 2),
-            grecv[7].astype(jnp.float32), 0.0,
+            grecv[5].astype(jnp.float32), 0.0,
         )
         above = jnp.where(left, mine, far)
         summed = jnp.where(left, neighbour_part(below, 0), neighbour_part(above, 1))
-        kept = jnp.where(left, wrecv[0, 0:width, :], wrecv[1, 0:width, :])
-        scale = jnp.where(
-            left[:8], wrecv[0, width:width + 8, :], wrecv[1, width:width + 8, :]
-        )[0:1]
-        ghosts = kept - scale * summed
-        return jnp.where(jnp.logical_or(from_lower, from_upper), ghosts, 0.0)
-
-    lmax = 2.0
-    lmin = 0.2
-    theta = (lmax + lmin) / 2.0
-    delta = (lmax - lmin) / 2.0
-    sigma = theta / delta
-    rho = 1.0 / sigma
+        return inside(mixed(wrecv) - mixed_scale(wrecv) * summed)
+
+    rho = 1.0 / SIGMA
     iterate = start
-    residual = (rhs_v[...] - own_part(start)) - ghost_part(0)
-    direction = residual * (inverse * (1.0 / theta))
+    residual = base - times(esend[0:width, :], wmat[...])
+    direction = residual * (inverse * (1.0 / THETA))
     for step in range(1, STEPS):
-        send_ghosts(step, direction)
-        if step == STEPS - 1:
-            remote(gsend.at[step], grecv.at[6], g_ss, g_rs.at[STEPS], upper2).start()
-            remote(gsend.at[step], grecv.at[7], g_ss, g_rs.at[STEPS], lower2).start()
+        last = step == STEPS - 1
+        if last:
+            send_ghosts(1, direction)
+            remote(gsend.at[1], grecv.at[4], g_ss, g_rs.at[2], upper2).start()
+            remote(gsend.at[1], grecv.at[5], g_ss, g_rs.at[2], lower2).start()
         iterate = iterate + direction
         rest = residual - own_part(direction)
-        rho_new = 1.0 / (2.0 * sigma - rho)
-        gain = (2.0 * rho_new / delta) * inverse
+        rho_new = 1.0 / (2.0 * SIGMA - rho)
+        gain = (2.0 * rho_new / DELTA) * inverse
         kept = (rho_new * rho) * direction + gain * rest
-        if step == STEPS - 1:
+        if last:
             wsend[0:width, :] = pack_ghosts(kept)
             wsend[width:width + 8, :] = pack_ghosts(jnp.broadcast_to(gain, (8, 128)))
             for way, peer in enumerate((upper, lower)):
                 remote(wsend, wrecv.at[way], w_ss, w_rs, peer).start()
-        ghosts = ghost_part(step)
+        ghosts = product(ghosts_of(1) if last else first_ghosts(), 128)
         direction = kept - gain * ghosts
         residual = rest - ghosts
         rho = rho_new
@@ -384,16 +434,19 @@
     out_copy.start()
     rest = residual - own_part(direction)
     wait_bytes(nrecv, n_rs)
-    wait_bytes(grecv.at[pl.ds(6, 2)], g_rs.at[STEPS])
+    wait_bytes(grecv.at[pl.ds(4, 2)], g_rs.at[2])
     wait_bytes(wrecv, w_rs)
-    residual = rest - product(next_ghosts(gsend[STEPS - 1].astype(jnp.float32)), 128)
+    residual = rest - product(next_ghosts(gsend[1].astype(jnp.float32)), 128)
 
     squares = jnp.sum((residual * residual).T, axis=0, keepdims=True)
     part = jnp.concatenate([squares, jnp.zeros((1, 128 - width), jnp.float32)], axis=1)
     for buf, ss, rs, here, count, peer in (
-        (red_p, red_p_ss, red_p_rs, plane, ng * nx, plane_peer),
+        (red_c, red_c_ss, red_c_rs, core, cores, core_peer),
+        (red_p, red_p_ss, red_p_rs, plane, chips, plane_peer),
         (red_z, red_z_ss, red_z_rs, z, nz, z_peer),
     ):
+        if count == 1:
+            continue
         buf[here] = part
         for n in range(1, count):
             remote(buf.at[here], buf.at[here], ss, rs, peer(n)).start()
@@ -411,7 +464,12 @@
     wait_bytes(grecv, g_ss)
     wait_bytes(nsend, n_ss)
     wait_bytes(wrecv, w_ss)
-    wait_bytes(red_p.at[pl.ds(0, ng * nx - 1)], red_p_ss)
+    wait_bytes(erecv, e_ss)
+    wait_bytes(yrecv, y_ss)
+    wait_bytes(vrecv, v_ss)
+    if cores > 1:
+        wait_bytes(red_c.at[pl.ds(0, 1)], red_c_ss)
+    wait_bytes(red_p.at[pl.ds(0, chips - 1)], red_p_ss)
     wait_bytes(red_z.at[pl.ds(0, nz - 1)], red_z_ss)
 
 
@@ -453,12 +511,20 @@
             vmem((2, nk - 1, 2, 2, 128), f32),
             vmem((2, nk - 1, 2, 2, 128), f32),
             vmem((256, 256), bf16),
-            vmem((STEPS, width, 128), bf16),
-            vmem((2 * STEPS + 2, width, 128), bf16),
+            vmem((2, width, 128), bf16),
+            vmem((6, width, 128), bf16),
             vmem((2, 128, 128), bf16),
             vmem((2, 128, 128), bf16),
             vmem((width + 8, 128), f32),
             vmem((2, width + 8, 128), f32),
+            vmem((width + 16, 256), bf16),
+            vmem((2, width + 16, 256), bf16),
+            vmem((2, 256, 256), bf16),
+            vmem((2, width, 128), f32),
+            vmem((2, 2, width, 128), f32),
+            vmem((width + 8, 128), f32),
+            vmem((2, width + 8, 128), f32),
+            vmem((2, 1, 128), f32),
             vmem((ng * nx, 1, 128), f32),
             vmem((nz, 1, 128), f32),
             vmem((width, 128), f32),
@@ -476,7 +542,15 @@
             dma,
             dma((2, nk - 1, 2)),
             dma,
-            dma((STEPS + 1,)),
+            dma((3,)),
+            dma,
+            dma,
+            dma,
+            dma,
+            dma,
+            dma,
+            dma,
+            dma,
             dma,
             dma,
             dma,

time: 62.2 us -> 60.8 us (0.977)
  Pallas kernels: 59.5 us -> 58.1 us
    pallas_call x1, Pallas kernels: 59.5 us -> 58.1 us  [shards(): pl.pallas_call(functools.partial(kernel, ng, nx, nz), out_shape=(jax.Shap...]
where the time goes in v6:
time: 60.8 us; the launch traced here: 60.6 us
  Pallas kernels  58.1 us (96%)
  local copies, waits for them, and re-layouts  1.84 us (3%)
  between operations  0.65 us (1%)
    pallas_call x1, Pallas kernels, shards(): pl.pallas_call(functools.partial(kernel, ng, nx, nz), out_shape=(jax.Shap...  58.1 us
    unnamed x4, local copies, waits for them, and re-layouts  1.84 us

profile of v6, /device:TPU:1, one launch (start us, length us, event | category | flops | bytes accessed | tf_op | source)
XLA Modules:
  0.0 60.6 jit_solution(9895829509148990781)
XLA Ops:
  0.6 58.1 %shard_map.95 = (f32[1,32,128]{2,1,0:T(8,128)}, f32[1,32]{1,0:T(1,128)}) custom-call(s32[1,54]{1,0:T(1,128)} %bitcast.2, s32[1,54]{1,0:T(1,128)} %rows_h.1, s32[1,54]{1,0:T(1,128)} %cols_h.1, s32[1,2]{1,0:T(1,128)} %ghost_h.1, bf16[1,54,64,64]{3,2,1,0:T(8,128)(2,1)} %tiles_h.1, f32[1,32,128]{2,1,0:T(8,128)} %rhs_h.1, f32[1,32,128]{2,1,0:T(8,128)} %start_h.1, ...), custom_call_target="tpu_custom_call" | custom-call | tf_op jit(solution)/shard_map/pallas_call | solution.py:483
  58.8 0.0 copy-start
  58.8 1.3 %copy.12 = f32[1,32,128]{2,1,0:T(8,128)} copy(f32[1,32,128]{2,1,0:T(8,128)} %get-tuple-element.8) | data formatting | bytes 32768
  60.1 0.0 copy-done
  60.1 0.5 copy.13
Async XLA Ops:
  58.8 1.3 %copy-start = (f32[1,32]{1,0:T(1,128)S(1)}, f32[1,32]{1,0:T(1,128)}, u32[]{:S(2)}) copy-start(f32[1,32]{1,0:T(1,128)} %get-tuple-element.5) | copy-start | bytes 388

commit v7 on v6

--- a/solution.py
+++ b/solution.py
@@ -60,6 +60,27 @@
     upper2 = {"dev": lax.rem(dev + 2, ndev)}
     lower2 = {"dev": lax.rem(dev + ndev - 2, ndev)}
 
+    barrier = pltpu.get_barrier_semaphore()
+    def ring_hops(n, count):
+        return min(n % count, count - n % count)
+
+    peers = [(ring_hops(j, nx) + 1, at(j, k)) for j in range(nx) for k in (-1, 1)]
+    peers += [(ring_hops(j, nx), at(j, 0)) for j in range(1, nx)]
+    peers += [(2, at(0, -2)), (2, at(0, 2))]
+    peers += [(ring_hops(j, nx) + 2, at(nx - j, 4 * (j % 2) - 2)) for j in range(1, nx)]
+    peers += [(2, upper), (2, lower), (3, upper2), (3, lower2)]
+    peers += [(0, core_peer(n)) for n in range(1, cores)]
+    peers += [
+        (ring_hops(n, nx) + ring_hops(n // nx, chips // nx), plane_peer(n))
+        for n in range(1, chips)
+    ]
+    peers = [peer for _, peer in sorted(peers, key=lambda entry: -entry[0])]
+
+    def greet(some):
+        for peer in some:
+            pl.semaphore_signal(barrier, inc=1, device_id=peer, device_id_type=MESH)
+
+    greet(peers[:10])
     fetches = [
         pltpu.make_async_copy(src, dst, in_sem.at[n])
         for n, (src, dst) in enumerate((
@@ -71,14 +92,7 @@
     for fetch in fetches:
         fetch.start()
 
-    barrier = pltpu.get_barrier_semaphore()
-    peers = [at(j, k) for j in range(nx) for k in (-1, 1)]
-    peers += [at(j, 0) for j in range(1, nx)] + [at(0, -2), at(0, 2)]
-    peers += [at(nx - j, 4 * (j % 2) - 2) for j in range(1, nx)]
-    peers += [upper, lower, upper2, lower2] + [core_peer(n) for n in range(1, cores)]
-    peers += [plane_peer(n) for n in range(1, chips)]
-    for peer in peers:
-        pl.semaphore_signal(barrier, inc=1, device_id=peer, device_id_type=MESH)
+    greet(peers[10:])
 
     lane = lax.broadcasted_iota(jnp.int32, (1, 128), 1)
     none = jnp.full((1, 128), -1, jnp.int32)
@@ -149,28 +163,42 @@
     def own_index(k, fam):
         return oc - 1 if k == 0 else 2 * (k - 1) + fam
 
-    order = list(range(1, nx)) + [0]
+    def over_x(body, count=nx):
+        def turn(i, _):
+            body(lax.rem(i + 1, nx))
+            return 0
+
+        lax.fori_loop(0, count, turn, 0)
+
+    def far_hops(j):
+        return 2 - 4 * lax.rem(j, 2)
+
+    def own_slots(j):
+        return own_slot + lax.rem(j + nx - 1, nx) * oc
+
+    def send_rows(first, count, peer):
+        rows = pl.ds(first, count)
+        remote(psend.at[rows], precv.at[rows], p_ss, p_rs, peer).start()
 
     def send_places():
-        for j in order:
-            spans = [
-                (leaf_row + (way * nx + j) * nk, nk, at(j, 1 - 2 * way)) for way in range(2)
-            ]
-            spans.append((far_row + j, 1, at(j, 2 - 4 * (j % 2))))
-            if j:
-                spans.append((j * oc, oc, at(j, 0)))
-            for first, count, peer in spans:
-                rows = pl.ds(first, count)
-                remote(psend.at[rows], precv.at[rows], p_ss, p_rs, peer).start()
+        def body(j):
+            for way in range(2):
+                send_rows(leaf_row + (way * nx + j) * nk, nk, at(j, 1 - 2 * way))
+            send_rows(far_row + j, 1, at(j, far_hops(j)))
+
+        over_x(body)
+        over_x(lambda j: send_rows(j * oc, oc, at(j, 0)), nx - 1)
 
     def send_far():
-        for j in order:
+        def body(j):
             remote(
-                bsend.at[j], frecv.at[j], b_ss, f_rs.at[j % 2], at(j, 2 - 4 * (j % 2))
+                bsend.at[j], frecv.at[j], b_ss, f_rs.at[lax.rem(j, 2)], at(j, far_hops(j))
             ).start()
 
+        over_x(body)
+
     def send_leaf(k):
-        for j in order:
+        def body(j):
             for way in range(2):
                 slot = leaf_slot + (way * nk + k) * nx + j
                 remote(
@@ -178,20 +206,23 @@
                     at(j, 1 - 2 * way),
                 ).start()
 
+        over_x(body)
+
     def send_own(k):
-        count = 1 if k == 0 else 2
-        for j in range(1, nx):
-            slot = own_slot + (j - 1) * oc + own_index(k, 0)
+        def body(j):
+            count = 1 if k == 0 else 2
             remote(
-                bsend.at[pl.ds(slot, count)], xown.at[j, pl.ds(own_index(k, 0), count)],
-                b_ss, o_rs.at[k], at(j, 0),
+                bsend.at[pl.ds(own_slots(j) + own_index(k, 0), count)],
+                xown.at[j, pl.ds(own_index(k, 0), count)], b_ss, o_rs.at[k], at(j, 0),
             ).start()
+
+        over_x(body, nx - 1)
 
     tab_copy.wait()
     fetches[4].wait()
     fetches[5].wait()
     start = start_v[...]
-    for j in range(nx):
+    def pack(j):
         o = owner_of(j, half)
         psend[far_row + j] = place(o)
         bsend[j] = pair(o)
@@ -202,13 +233,12 @@
                 bsend[leaf_slot + (way * nk + k) * nx + j] = pair(o)
             for fam in range(1 if k == 0 else 2):
                 o = owner_of(j, own_step(fam, k))
-                n = own_index(k, fam)
-                if j:
-                    psend[j * oc + n] = place(o)
-                    bsend[own_slot + (j - 1) * oc + n] = pair(o)
-                else:
-                    precv[n] = place(o)
-                    xown[0, n] = pair(o)
+                psend[j * oc + own_index(k, fam)] = place(o)
+                bsend[own_slots(j) + own_index(k, fam)] = pair(o)
+
+    over_x(pack)
+    precv[0:oc] = psend[0:oc]
+    xown[0] = bsend[own_slot + (nx - 1) * oc:own_slot + nx * oc]
 
     pl.semaphore_wait(barrier, len(peers))
     send_far()
@@ -232,30 +262,36 @@
             out.append(value + jnp.where(row_swapped == target, swapped, 0.0))
         return tuple(out)
 
+    def own_arrived(k):
+        count = 1 if k == 0 else 2
+        wait_bytes(xown.at[pl.ds(1, nx - 1), pl.ds(own_index(k, 0), count)], o_rs.at[k])
+
     def dense(n, k, fam, leaves, far):
         acc = tuple(jnp.zeros((64, 128), jnp.float32) for _ in range(CH))
         if far:
-            wait_bytes(frecv.at[pl.ds(0, len(far))], f_rs.at[fam])
-        for j in far:
-            acc = add_pair(acc, frecv[j], precv[far_row + j])
+            wait_bytes(frecv.at[pl.ds(0, nx // 2)], f_rs.at[fam])
+            for i in range(nx // 2):
+                acc = add_pair(acc, frecv[2 * i + fam], precv[far_row + 2 * i + fam])
         for way, kk in leaves:
             wait_bytes(lrecv.at[way, kk], l_rs.at[way, kk])
             for j in range(nx):
                 row = leaf_row + (way * nx + j) * nk + kk
                 acc = add_pair(acc, lrecv[way, kk, j], precv[row])
-        if fam == 0:
-            count = 1 if k == 0 else 2
-            wait_bytes(
-                xown.at[pl.ds(1, nx - 1), pl.ds(own_index(k, 0), count)], o_rs.at[k]
-            )
         for j in range(nx):
             i = own_index(k, fam)
             acc = add_pair(acc, xown[j, i], precv[j * oc + i])
         for c in range(CH):
             dmat[n, c] = acc[c]
 
+    def both_ways(body):
+        def turn(way, _):
+            body(way)
+            return 0
+
+        lax.fori_loop(0, 2, turn, 0)
+
     def chain_copies(way, s, h):
-        peer = z_peer(2 if way == 0 else -2)
+        peer = z_peer(2 - 4 * way)
         n = s - 1
         return (
             remote(ssend.at[way, n, h], srecv.at[way, n, h], s_ss, s_rs.at[way, n, h], peer),
@@ -297,20 +333,32 @@
         return jnp.where(from_upper, grecv[2 * n + 1].astype(jnp.float32), ghosts)
 
     for s in range(1, nk):
-        for way in range(2):
-            far = [j for j in range(nx) if j % 2 == way] if s == 1 else []
-            dense(way, s, way, [(way, s - 1)], far)
-        for h in range(2):
-            for way in range(2):
-                values = [dmat[way, h * 2 + cp] for cp in range(2)]
-                if s > 1:
-                    for copy in chain_copies(way, s - 1, h):
-                        copy.wait_recv()
-                    values = [values[cp] + arrived(way, s - 1, h, cp) for cp in range(2)]
-                send_half(way, s, h, values)
-                if s == nk - 1:
-                    for cp in range(2):
-                        split(pmat.at[way], h, cp, values[cp])
+        def form(way):
+            dense(way, s, way, [(way, s - 1)], s == 1)
+
+        def pass_on(way, h):
+            values = [dmat[way, h * 2 + cp] for cp in range(2)]
+            if s > 1:
+                for copy in chain_copies(way, s - 1, h):
+                    copy.wait_recv()
+                values = [values[cp] + arrived(way, s - 1, h, cp) for cp in range(2)]
+            send_half(way, s, h, values)
+            if s == nk - 1:
+                for cp in range(2):
+                    split(pmat.at[way], h, cp, values[cp])
+
+        def first(way):
+            form(way)
+            for h in range(2):
+                pass_on(way, h)
+
+        own_arrived(s)
+        if s == 1:
+            both_ways(first)
+        else:
+            both_ways(form)
+            for h in range(2):
+                both_ways(functools.partial(pass_on, h=h))
         if s == 1:
             ghosts = ghosts_of(0)
             esend[0:width, 0:128] = start.astype(jnp.bfloat16)
@@ -324,7 +372,7 @@
             send_leaf(s + 1)
             send_own((s + 2) % nk)
     wait_bytes(erecv, e_rs)
-    for way in range(2):
+    def pass_products(way):
         part = times(erecv[way, 0:width, :], pmat[way])
         turned = erecv[way, width:width + 16, 0:128].astype(jnp.float32)[0:1]
         ysend[way] = jnp.where(turned > 0.5, part, pltpu.roll(part, 64, 1))
@@ -335,6 +383,8 @@
                 {"dev": lax.rem(first + 1 - 2 * side + ndev, ndev)},
             ).start()
 
+    both_ways(pass_products)
+    own_arrived(0)
     dense(0, 0, 0, [(0, nk - 1), (1, nk - 1)], [])
     fetches[6].wait()
     fetches[7].wait()
@@ -458,7 +508,7 @@
 
     out_copy.wait()
     wait_bytes(psend.at[pl.ds(oc, far_row + nx - oc)], p_ss)
-    wait_bytes(bsend, b_ss)
+    wait_bytes(bsend.at[pl.ds(0, own_slot + (nx - 1) * oc)], b_ss)
     wait_bytes(qsend, q_ss)
     wait_bytes(ssend, s_ss)
     wait_bytes(grecv, g_ss)
@@ -501,7 +551,7 @@
             smem((8, 128), i32),
             vmem((nx * (4 * nk), 1, 128), i32),
             vmem((nx * (4 * nk), 1, 128), i32),
-            vmem((nx + 2 * nk * nx + (nx - 1) * (2 * nk - 1), 64, 128), bf16),
+            vmem((nx * 4 * nk, 64, 128), bf16),
             vmem((nx, 2 * nk - 1, 64, 128), bf16),
             vmem((2, nk, nx, 64, 128), bf16),
             vmem((nx, 64, 128), bf16),

time: 60.8 us -> 60.8 us (level)
  no operation moved by 1% of the time
where the time goes in v7:
time: 60.8 us; the launch traced here: 60.6 us
  Pallas kernels  58.1 us (96%)
  local copies, waits for them, and re-layouts  1.84 us (3%)
  between operations  0.65 us (1%)
    pallas_call x1, Pallas kernels, shards(): pl.pallas_call(functools.partial(kernel, ng, nx, nz), out_shape=(jax.Shap...  58.1 us
    unnamed x4, local copies, waits for them, and re-layouts  1.84 us

profile of v7, /device:TPU:1, one launch (start us, length us, event | category | flops | bytes accessed | tf_op | source)
XLA Modules:
  0.0 60.6 jit_solution(1064644018396060377)
XLA Ops:
  0.6 58.1 %shard_map.95 = (f32[1,32,128]{2,1,0:T(8,128)}, f32[1,32]{1,0:T(1,128)}) custom-call(s32[1,54]{1,0:T(1,128)} %bitcast.2, s32[1,54]{1,0:T(1,128)} %rows_h.1, s32[1,54]{1,0:T(1,128)} %cols_h.1, s32[1,2]{1,0:T(1,128)} %ghost_h.1, bf16[1,54,64,64]{3,2,1,0:T(8,128)(2,1)} %tiles_h.1, f32[1,32,128]{2,1,0:T(8,128)} %rhs_h.1, f32[1,32,128]{2,1,0:T(8,128)} %start_h.1, ...), custom_call_target="tpu_custom_call" | custom-call | tf_op jit(solution)/shard_map/pallas_call | solution.py:533
  58.8 0.0 copy-start
  58.8 1.3 %copy.12 = f32[1,32,128]{2,1,0:T(8,128)} copy(f32[1,32,128]{2,1,0:T(8,128)} %get-tuple-element.8) | data formatting | bytes 32768
  60.1 0.0 copy-done
  60.1 0.5 copy.13
Async XLA Ops:
  58.8 1.3 %copy-start = (f32[1,32]{1,0:T(1,128)S(1)}, f32[1,32]{1,0:T(1,128)}, u32[]{:S(2)}) copy-start(f32[1,32]{1,0:T(1,128)} %get-tuple-element.5) | copy-start | bytes 388

commit v8 on v7

--- a/solution.py
+++ b/solution.py
@@ -241,13 +241,13 @@
     xown[0] = bsend[own_slot + (nx - 1) * oc:own_slot + nx * oc]
 
     pl.semaphore_wait(barrier, len(peers))
+    send_ghosts(0, start)
     send_far()
     send_leaf(0)
     send_own(1)
     send_places()
     send_leaf(1)
     send_own(2 % nk)
-    send_ghosts(0, start)
 
     right_half = (lane >= 64).astype(jnp.int32)
 

time: 60.8 us -> 60.4 us (level)
  no operation moved by 1% of the time
where the time goes in v8:
time: 60.4 us; the launch traced here: 60.2 us
  Pallas kernels  57.8 us (96%)
  local copies, waits for them, and re-layouts  1.84 us (3%)
  between operations  0.65 us (1%)
    pallas_call x1, Pallas kernels, shards(): pl.pallas_call(functools.partial(kernel, ng, nx, nz), out_shape=(jax.Shap...  57.8 us
    unnamed x4, local copies, waits for them, and re-layouts  1.84 us

profile of v8, /device:TPU:1, one launch (start us, length us, event | category | flops | bytes accessed | tf_op | source)
XLA Modules:
  0.0 60.2 jit_solution(10089767804663038605)
XLA Ops:
  0.6 57.8 %shard_map.95 = (f32[1,32,128]{2,1,0:T(8,128)}, f32[1,32]{1,0:T(1,128)}) custom-call(s32[1,54]{1,0:T(1,128)} %bitcast.2, s32[1,54]{1,0:T(1,128)} %rows_h.1, s32[1,54]{1,0:T(1,128)} %cols_h.1, s32[1,2]{1,0:T(1,128)} %ghost_h.1, bf16[1,54,64,64]{3,2,1,0:T(8,128)(2,1)} %tiles_h.1, f32[1,32,128]{2,1,0:T(8,128)} %rhs_h.1, f32[1,32,128]{2,1,0:T(8,128)} %start_h.1, ...), custom_call_target="tpu_custom_call" | custom-call | tf_op jit(solution)/shard_map/pallas_call | solution.py:533
  58.4 0.0 copy-start
  58.4 1.3 %copy.12 = f32[1,32,128]{2,1,0:T(8,128)} copy(f32[1,32,128]{2,1,0:T(8,128)} %get-tuple-element.8) | data formatting | bytes 32768
  59.7 0.0 copy-done
  59.7 0.5 copy.13
Async XLA Ops:
  58.4 1.3 %copy-start = (f32[1,32]{1,0:T(1,128)S(1)}, f32[1,32]{1,0:T(1,128)}, u32[]{:S(2)}) copy-start(f32[1,32]{1,0:T(1,128)} %get-tuple-element.5) | copy-start | bytes 388

commit v9 on v8

--- a/solution.py
+++ b/solution.py
@@ -290,28 +290,30 @@
 
         lax.fori_loop(0, 2, turn, 0)
 
-    def chain_copies(way, s, h):
+    def chain_copies(way, s, h, cp):
         peer = z_peer(2 - 4 * way)
-        n = s - 1
+        at_n = (way, s - 1, h, cp)
         return (
-            remote(ssend.at[way, n, h], srecv.at[way, n, h], s_ss, s_rs.at[way, n, h], peer),
-            remote(qsend.at[way, n, h], qrecv.at[way, n, h], q_ss, q_rs.at[way, n, h], peer),
+            remote(ssend.at[at_n], srecv.at[at_n], s_ss, s_rs.at[at_n], peer),
+            remote(qsend.at[at_n], qrecv.at[at_n], q_ss, q_rs.at[at_n], peer),
         )
 
-    def send_half(way, s, h, values):
-        for cp in range(2):
-            most = jnp.maximum(jnp.max(jnp.abs(values[cp]), axis=0, keepdims=True), 1e-30)
-            scaled = jnp.round(values[cp] * (32767.0 / most))
-            qsend[way, s - 1, h, cp] = scaled.astype(jnp.int32).astype(jnp.int16)
-            ssend[way, s - 1, h, cp:cp + 1, :] = most * (1.0 / 32767.0)
-        for copy in chain_copies(way, s, h):
+    def send_chunk(way, s, h, cp, value):
+        most = jnp.maximum(jnp.max(jnp.abs(value), axis=0, keepdims=True), 1e-30)
+        scaled = jnp.round(value * (32767.0 / most))
+        qsend[way, s - 1, h, cp] = scaled.astype(jnp.int32).astype(jnp.int16)
+        ssend[way, s - 1, h, cp] = most * (1.0 / 32767.0)
+        for copy in chain_copies(way, s, h, cp):
             copy.start()
 
     def arrived(way, s, h, cp):
+        for copy in chain_copies(way, s, h, cp):
+            copy.wait_recv()
         whole = qrecv[way, s - 1, h, cp].astype(jnp.int32).astype(jnp.float32)
-        return whole * srecv[way, s - 1, h, cp:cp + 1, :]
+        return whole * srecv[way, s - 1, h, cp]
 
     wait_bytes(precv.at[pl.ds(oc, far_row + nx - oc)], p_rs)
+
     def split(matrix, h, cp, value):
         high = value.astype(jnp.bfloat16)
         low = (value - high.astype(jnp.float32)).astype(jnp.bfloat16)
@@ -336,29 +338,26 @@
         def form(way):
             dense(way, s, way, [(way, s - 1)], s == 1)
 
-        def pass_on(way, h):
-            values = [dmat[way, h * 2 + cp] for cp in range(2)]
+        def pass_on(way, h, cp):
+            value = dmat[way, h * 2 + cp]
             if s > 1:
-                for copy in chain_copies(way, s - 1, h):
-                    copy.wait_recv()
-                values = [values[cp] + arrived(way, s - 1, h, cp) for cp in range(2)]
-            send_half(way, s, h, values)
+                value = value + arrived(way, s - 1, h, cp)
+            send_chunk(way, s, h, cp, value)
             if s == nk - 1:
-                for cp in range(2):
-                    split(pmat.at[way], h, cp, values[cp])
+                split(pmat.at[way], h, cp, value)
 
         def first(way):
             form(way)
-            for h in range(2):
-                pass_on(way, h)
+            for c in range(CH):
+                pass_on(way, c // 2, c % 2)
 
         own_arrived(s)
         if s == 1:
             both_ways(first)
         else:
             both_ways(form)
-            for h in range(2):
-                both_ways(functools.partial(pass_on, h=h))
+            for c in range(CH):
+                both_ways(functools.partial(pass_on, h=c // 2, cp=c % 2))
         if s == 1:
             ghosts = ghosts_of(0)
             esend[0:width, 0:128] = start.astype(jnp.bfloat16)
@@ -402,8 +401,6 @@
     for h in range(2):
         values = [dmat[0, h * 2 + cp] for cp in range(2)]
         for way in range(2):
-            for copy in chain_copies(way, nk - 1, h):
-                copy.wait_recv()
             values = [values[cp] + arrived(way, nk - 1, h, cp) for cp in range(2)]
         for cp in range(2):
             split(wmat, h, cp, values[cp])
@@ -558,8 +555,8 @@
             vmem((2, CH, 64, 128), f32),
             vmem((2, nk - 1, 2, 2, 64, 128), i16),
             vmem((2, nk - 1, 2, 2, 64, 128), i16),
-            vmem((2, nk - 1, 2, 2, 128), f32),
-            vmem((2, nk - 1, 2, 2, 128), f32),
+            vmem((2, nk - 1, 2, 2, 1, 128), f32),
+            vmem((2, nk - 1, 2, 2, 1, 128), f32),
             vmem((256, 256), bf16),
             vmem((2, width, 128), bf16),
             vmem((6, width, 128), bf16),
@@ -588,9 +585,9 @@
             dma((2, nk)),
             dma((2,)),
             dma,
-            dma((2, nk - 1, 2)),
-            dma,
-            dma((2, nk - 1, 2)),
+            dma((2, nk - 1, 2, 2)),
+            dma,
+            dma((2, nk - 1, 2, 2)),
             dma,
             dma((3,)),
             dma,

time: 60.4 us -> 60.7 us (level)
  no operation moved by 1% of the time
where the time goes in v9:
time: 60.7 us; the launch traced here: 60.6 us
  Pallas kernels  58.1 us (96%)
  local copies, waits for them, and re-layouts  1.84 us (3%)
  between operations  0.65 us (1%)
    pallas_call x1, Pallas kernels, shards(): pl.pallas_call(functools.partial(kernel, ng, nx, nz), out_shape=(jax.Shap...  58.1 us
    unnamed x4, local copies, waits for them, and re-layouts  1.84 us

profile of v9, /device:TPU:1, one launch (start us, length us, event | category | flops | bytes accessed | tf_op | source)
XLA Modules:
  0.0 60.6 jit_solution(17496655289072575126)
XLA Ops:
  0.6 58.1 %shard_map.95 = (f32[1,32,128]{2,1,0:T(8,128)}, f32[1,32]{1,0:T(1,128)}) custom-call(s32[1,54]{1,0:T(1,128)} %bitcast.2, s32[1,54]{1,0:T(1,128)} %rows_h.1, s32[1,54]{1,0:T(1,128)} %cols_h.1, s32[1,2]{1,0:T(1,128)} %ghost_h.1, bf16[1,54,64,64]{3,2,1,0:T(8,128)(2,1)} %tiles_h.1, f32[1,32,128]{2,1,0:T(8,128)} %rhs_h.1, f32[1,32,128]{2,1,0:T(8,128)} %start_h.1, ...), custom_call_target="tpu_custom_call" | custom-call | tf_op jit(solution)/shard_map/pallas_call | solution.py:530
  58.7 0.0 copy-start
  58.7 1.3 %copy.12 = f32[1,32,128]{2,1,0:T(8,128)} copy(f32[1,32,128]{2,1,0:T(8,128)} %get-tuple-element.8) | data formatting | bytes 32768
  60.0 0.0 copy-done
  60.0 0.5 copy.13
Async XLA Ops:
  58.7 1.3 %copy-start = (f32[1,32]{1,0:T(1,128)S(1)}, f32[1,32]{1,0:T(1,128)}, u32[]{:S(2)}) copy-start(f32[1,32]{1,0:T(1,128)} %get-tuple-element.5) | copy-start | bytes 388
